TPU v7x, 512 devices: a whole 4x8x8 slice. The times are simulated.
512 devices in a mesh: wide: 64 (over z_lo, x, y), narrow: 8 (over z_hi, core).
Axes of the slice: x: 4, y: 8, z: 8 (z_hi: 4, z_lo: 2; z = z_hi * 2 + z_lo), core: 2. Of those that a mesh axis runs over, the one named last changes fastest.
Arguments:
- points: bfloat16 [65536, 256], P(('wide', 'narrow')), may hold values from -8 to 8
- log_point_weight: float32 [65536], P(('wide', 'narrow')), may hold values from -4 to 4
- potential: float32 [65536], P(('wide', 'narrow')), may hold values from -12 to 503
Outputs:
- new_potential: float32 [65536], P(('wide', 'narrow'))
- residual_norm: float32 [], replicated
All inputs are finite; a program needn't handle non-finite values.
Results may differ from a plain program's by a relative error of at most 0.0003.
Values may be sent and summed in bfloat16 or wider, within the bound.
No kernel may reach another device: no remote copies, remote signals or barrier semaphores. Data moves between devices by JAX's collectives and lax.ppermute only.
A program may use at most 64 MiB of HBM per device.

v0:
```python
import math

import jax
import jax.numpy as jnp
from jax import lax
from jax.sharding import PartitionSpec as P

entropic_epsilon = 2.0


def merged(value, axis, join):
    pieces = lax.all_gather(value, axis)
    head = pieces[0]
    tail = pieces[1:]
    total, _ = lax.scan(lambda total, share: (join(total, share), None), head, tail)
    return total


def absorb_columns(row_points, carry, column_points, column_shift):
    column_count = column_points.shape[0]
    block_width = math.gcd(column_count, 512)
    point_blocks = column_points.reshape(
        column_count // block_width, block_width, column_points.shape[1]
    )
    shift_blocks = column_shift.reshape(column_count // block_width, block_width)

    def advance(state, column_block):
        running_max, running_total = state
        block_points, block_offset_amount = column_block
        inner_products = jnp.einsum(
            "pf,qf->pq", row_points, block_points, preferred_element_type=jnp.float32
        )
        kernel_scores = block_offset_amount[None, :] + inner_products / entropic_epsilon
        highest = jnp.maximum(running_max, jnp.max(kernel_scores, axis=1))
        running_total = running_total * jnp.exp(running_max - highest) + jnp.sum(
            jnp.exp(kernel_scores - highest[:, None]), axis=1
        )
        return ((highest, running_total), None)

    result, unused = lax.scan(advance, carry, (point_blocks, shift_blocks))
    return result


def pair_combine(left, right):
    larger = jnp.maximum(left, right)
    return larger + jnp.log(jnp.exp(left - larger) + jnp.exp(right - larger))


def finish_narrow(partial_value, local_rows):
    combined = merged(partial_value, "narrow", pair_combine)
    return lax.dynamic_slice_in_dim(combined, lax.axis_index("narrow") * local_rows, local_rows)


def per_device(points, log_point_weight, potential):
    squared_norms = jnp.sum(jnp.square(points.astype(jnp.float32)), axis=1)
    offset_scores = (
        log_point_weight + potential / entropic_epsilon - 0.5 * squared_norms / entropic_epsilon
    )
    local_rows = points.shape[0]
    row_points = lax.all_gather(points, "narrow", axis=0, tiled=True)
    group_rows = row_points.shape[0]
    initial = (jnp.full((group_rows,), -1e30, jnp.float32), jnp.zeros((group_rows,), jnp.float32))
    piece_points = lax.all_gather(points.astype(jnp.float32), "wide", axis=0, tiled=True)
    piece_shift = lax.all_gather(offset_scores, "wide", axis=0, tiled=True)
    running_max, running_total = absorb_columns(
        row_points, initial, piece_points.astype(jnp.bfloat16), piece_shift
    )
    partial_value = running_max + jnp.log(running_total)
    log_normalizer = finish_narrow(partial_value, local_rows)
    refreshed_potential = 0.5 * squared_norms - entropic_epsilon * log_normalizer
    new_potential = 0.5 * (potential + refreshed_potential)
    change = refreshed_potential - potential
    total_change = lax.psum(jnp.sum(change * change), ("wide", "narrow"))
    point_count = local_rows * lax.axis_size(("wide", "narrow"))
    residual_norm = jnp.sqrt(total_change / point_count + 1e-06)
    return (new_potential, residual_norm)


def solution(mesh):
    in_specs = (P(("wide", "narrow"), None), P(("wide", "narrow")), P(("wide", "narrow")))
    out_specs = (P(("wide", "narrow")), P())
    return jax.shard_map(
        per_device, mesh=mesh, in_specs=in_specs, out_specs=out_specs, check_vma=False
    )
```

profile of v0, /device:TPU:1, one launch (start us, length us, event | category | flops | bytes accessed | tf_op | source)
XLA Modules:
  0.0 478.2 jit_solution(3160840123513408432)
XLA Ops:
  7.2 0.7 all-gather.4.cloned.1.call-update
  7.9 0.9 multiply_reduce_fusion
  8.9 0.7 subtract_bitcast_fusion
  9.6 131.0 %all-gather.1 = f32[64,1,128]{2,1,0:T(1,128)S(1)} all-gather(f32[1,1,128]{2,1,0:T(1,128)S(1)} %subtract_bitcast_fusion), channel_id=1, replica_groups=mesh['wide'=64,'narrow'=8] {'wide'}, dimensions={0}, use_global_device_ids=true | all-gather | bytes 33280 | tf_op jit(solution)/shard_map/all_gather | solution.py:64
  140.5 0.5 broadcast.43
  141.0 0.7 reduce.5
  141.8 47.8 %all_gather.17 = bf16[1024,256]{1,0:T(8,128)(2,1)S(1)} all-gather(bf16[128,256]{1,0:T(8,128)(2,1)} %param.7), channel_id=1, replica_groups=mesh['wide'=64,'narrow'=8] {'narrow'}, dimensions={0}, use_global_device_ids=true | all-gather | bytes 589824 | tf_op jit(solution)/shard_map/all_gather | solution.py:60
  189.5 90.5 %all-gather.4.cloned.1.call-done = bf16[8192,256]{1,0:T(8,128)(2,1)} async-done(((bf16[128,256]{1,0:T(8,128)(2,1)}), bf16[8192,256]{1,0:T(8,128)(2,1)}) %all-gather.4.cloned.1.call-update) | async-done | bytes 4194320 | tf_op jit(solution)/shard_map/all_gather | solution.py:63
  280.0 32.2 %while.24 = (s32[]{:T(128)}, f32[1024]{0:T(1024)S(1)}, f32[1024]{0:T(1024)S(1)}, f32[16,512]{1,0:T(8,128)S(1)}, bf16[16,512,256]{2,1,0:T(8,128)(2,1)}, /*index=5*/bf16[1024,256]{1,0:T(8,128)(2,1)S(1)}, s32[]{:T(128)}, s32[]{:T(128)}) while((s32[]{:T(128)}, f32[1024]{0:T(1024)S(1)}, f32[1024]{0:T(1024)S(1)}, ...), condition=%wide.region_4.5_spmd.clone, body=%wide.region_1.4_spmd.clone.sunk | while | flops 272110592 | bytes 5042788 | solution.py:40
  280.0 1.4 fusion.12
  281.5 0.5 exponential_reduce_fusion.2
  282.0 1.4 fusion.12
  284.0 1.4 fusion.12
  286.0 1.4 fusion.12
  288.1 1.4 fusion.12
  290.1 1.4 fusion.12
  291.5 0.5 exponential_reduce_fusion.2
  292.1 1.4 fusion.12
  294.1 1.4 fusion.12
  296.1 1.4 fusion.12
  298.1 1.4 fusion.12
  300.1 1.4 fusion.12
  302.1 1.4 fusion.12
  304.2 1.4 fusion.12
  305.6 0.5 exponential_reduce_fusion.2
  306.2 1.4 fusion.12
  308.2 1.4 fusion.12
  310.2 1.4 fusion.12
  312.2 59.1 %all-gather = f32[8192]{0:T(1024)S(1)} all-gather(f32[1024]{0:T(1024)S(1)} %log_add_fusion.1), channel_id=2, replica_groups=mesh['wide'=64,'narrow'=8] {'narrow'}, dimensions={0}, use_global_device_ids=true | all-gather | bytes 36864 | tf_op jit(solution)/shard_map/all_gather | solution.py:12
  371.7 0.7 multiply_reduce_fusion.1
  372.4 96.6 %psum.7 = f32[]{:T(128)} all-reduce(f32[]{:T(128)} %get-tuple-element.94), channel_id=1, replica_groups=mesh['wide'=64,'narrow'=8] {'wide','narrow'}, use_global_device_ids=true, to_apply=%region_8.9 | all-reduce | flops 1 | bytes 8 | tf_op jit(solution)/shard_map/psum | solution.py:73
  469.7 0.5 add_multiply_fusion
  (102 shorter events, 7.3 us)
Async XLA Ops:
  7.2 272.8 %all-gather.4.cloned.1.call-start = ((), (), s32[]{:S(2)}) async-start(), calls=%async_computation | async-start | bytes 4259840 | tf_op jit(solution)/shard_map/all_gather | solution.py:63
  280.0 91.7 %copy-start = (f32[128]{0:T(128)S(1)}, f32[128]{0:T(128)}, u32[]{:S(2)}) copy-start(f32[128]{0:T(128)} %param.9) | copy-start | bytes 1540
Sparse Core Ops, SparseCore 0:
  10.1 269.8 all-gather.3
where the time goes:
time: 479 us; the launch traced here: 478 us
  blocking collectives  334 us (70%)
  waiting for transfers between devices  91.1 us (19%)
  matrix products  23 us (5%)
  between operations  15.9 us (3%)
  other arithmetic  11.6 us (2%)
    all_gather x1, blocking collectives, per_device(): piece_shift = lax.all_gather(offset_scores, 'wide', axis=0, tiled=True)  131 us
    psum x1, blocking collectives, per_device(): total_change = lax.psum(jnp.sum(change * change), ('wide', 'narrow'))  96.6 us
    all_gather x1, waiting for transfers between devices, per_device(): lax.all_gather(points.astype(jnp.float32), 'wide', axis=0, tiled=True)  90.5 us
    all_gather x1, blocking collectives, merged(): pieces = lax.all_gather(value, axis)  59.1 us
    all_gather x1, blocking collectives, per_device(): row_points = lax.all_gather(points, 'narrow', axis=0, tiled=True)  47.8 us
    dot_general x16, matrix products, advance(): jnp.einsum('pf,qf->pq', row_points, block_points, preferred_element_type=...  23 us
  transfers between devices with their start and end apart: 1, of which 1 were waited for; matrix products, arithmetic and copies ran while one was open for 1% of the time, Pallas kernels for 0%

commit v1 on v0

v1 whole, which is shorter than its diff:
```python
import math

import jax
import jax.numpy as jnp
from jax import lax
from jax.experimental import pallas as pl
from jax.experimental.pallas import tpu as pltpu
from jax.sharding import PartitionSpec as P

LOG2E = math.log2(math.e)
LN2 = math.log(2.0)
AXES = ("wide", "narrow")
SHAPE = (2, 2, 2, 8, 4, 2)
MEMBERS = 16
LOCAL = 128
TAIL = 16
MESSAGE = 2 * LOCAL + TAIL
VMEM = 56 * 1024 * 1024


def index(z_lo, x_hi, x_lo, y, z_hi, core):
    where = 0
    for size, at in zip(SHAPE, (z_lo, x_hi, x_lo, y, z_hi, core)):
        where = where * size + at
    return where


def row_groups(cores):
    return [
        [index(a, b, c, y, h, core) for c in range(2) for y in range(8)]
        for a in range(2)
        for b in range(2)
        for h in range(4)
        for core in cores
    ]


def column_groups(cores):
    return [
        [index(a, b, c, y, h, core) for b in range(2) for h in range(4) for a in range(2)]
        for c in range(2)
        for y in range(8)
        for core in cores
    ]


def remaining_groups():
    return [
        [
            index(a, b, c, y, h, core)
            for b in range(2)
            for h in range(4)
            for a in range(2)
            for core in range(2)
        ]
        for c in range(2)
        for y in range(8)
    ]


def three_terms(value):
    high = value.astype(jnp.bfloat16).astype(jnp.float32)
    rest = value - high
    middle = rest.astype(jnp.bfloat16).astype(jnp.float32)
    return high, middle, rest - middle


def pack_kernel(points_ref, weight_ref, potential_ref, out_ref):
    points = points_ref[...]
    wide = points.astype(jnp.float32)
    square = wide * wide
    high = square.astype(jnp.bfloat16)
    low = (square - high.astype(jnp.float32)).astype(jnp.bfloat16)
    ones = jnp.ones((8, points.shape[1]), jnp.bfloat16)
    dims = (((1,), (1,)), ((), ()))
    norms = lax.dot_general(ones, high, dims, preferred_element_type=jnp.float32)
    norms = norms + lax.dot_general(ones, low, dims, preferred_element_type=jnp.float32)
    norms = norms[:1]
    potential = potential_ref[...]
    offset = weight_ref[...] + 0.5 * potential - 0.25 * norms
    rows = [
        jnp.concatenate([a, b], axis=1)
        for a, b in zip(three_terms(offset * LOG2E), three_terms(0.5 * norms - potential))
    ]
    half = jnp.concatenate(rows + [jnp.zeros((5, 2 * LOCAL), jnp.float32)], axis=0)
    out_ref[:LOCAL] = points
    out_ref[LOCAL:] = jnp.concatenate([half, half], axis=0).astype(jnp.bfloat16)


def spread_kernel(pair_ref, out_ref):
    stride = LOCAL + TAIL
    first, second = pair_ref[LOCAL:stride], pair_ref[stride + LOCAL :]
    row = lax.broadcasted_iota(jnp.int32, first.shape, 0)
    tail = jnp.where(row < 8, first.astype(jnp.float32), second.astype(jnp.float32))
    tail = tail.astype(jnp.bfloat16)
    for member in range(MEMBERS):
        out_ref[member, :LOCAL] = pair_ref[:LOCAL]
        out_ref[member, LOCAL : 2 * LOCAL] = pair_ref[stride : stride + LOCAL]
        out_ref[member, 2 * LOCAL :] = tail


def pairs_kernel(
    core_ref, own_ref, other_ref, sum_ref, base_ref, rows, row_tail, columns, offsets, sems
):
    core = core_ref[0]

    def copies(row_source, column_source):
        return (
            pltpu.make_async_copy(
                row_source.at[:, pl.ds(pl.multiple_of(core * LOCAL, LOCAL), LOCAL)], rows, sems.at[0]
            ),
            pltpu.make_async_copy(row_source.at[:, pl.ds(2 * LOCAL, TAIL)], row_tail, sems.at[1]),
            pltpu.make_async_copy(column_source, columns, sems.at[2]),
        )

    @pl.when(core == 0)
    def _():
        for copy in copies(own_ref, other_ref):
            copy.start()

    @pl.when(core == 1)
    def _():
        for copy in copies(other_ref, own_ref):
            copy.start()

    for copy in copies(own_ref, other_ref):
        copy.wait()

    tails = row_tail[...].astype(jnp.float32)[:, :, LOCAL:]
    half = lax.broadcasted_iota(jnp.int32, tails.shape, 1) // 8
    base_ref[...] = jnp.sum(jnp.where(half == core, tails, 0.0), axis=1)

    half = lax.broadcasted_iota(jnp.int32, (TAIL, LOCAL), 0) // 8
    for member in range(MEMBERS):
        tail = columns[member, 2 * LOCAL :, :LOCAL]
        for side in range(2):
            pick = jnp.where(half == side, 1.0, 0.0).astype(jnp.bfloat16)
            offsets[member, side * LOCAL : (side + 1) * LOCAL] = lax.dot_general(
                tail, pick, (((0,), (0,)), ((), ())), preferred_element_type=jnp.float32
            )

    scale = 0.5 * LOG2E

    def row_step(step, unused):
        mine = rows[pl.ds(2 * step, 2)].reshape(2 * LOCAL, -1)
        highest = total = None
        for member in range(MEMBERS):
            inner = lax.dot_general(
                columns[member, : 2 * LOCAL],
                mine,
                (((1,), (1,)), ((), ())),
                preferred_element_type=jnp.float32,
            )
            shift = offsets[member]
            score = inner * scale + jnp.concatenate([shift, shift], axis=1)
            score = score.reshape(2 * LOCAL // 8, 8, 2 * LOCAL)
            top = jnp.max(score, axis=0)
            if member:
                top = jnp.maximum(top, highest)
            part = jnp.sum(jnp.exp2(score - top[None]), axis=0)
            total = part if member == 0 else part + total * jnp.exp2(highest - top)
            highest = top
        top = jnp.max(highest, axis=0, keepdims=True)
        total = jnp.sum(total * jnp.exp2(highest - top), axis=0, keepdims=True)
        value = top + jnp.log2(total)
        sum_ref[pl.ds(2 * step, 1)] = value[:, :LOCAL]
        sum_ref[pl.ds(2 * step + 1, 1)] = value[:, LOCAL:]
        return unused

    lax.fori_loop(0, MEMBERS // 2, row_step, 0)


def finish_kernel(place_ref, parts_ref, base_ref, potential_ref, new_ref, change_ref):
    parts = parts_ref[...]
    top = jnp.max(parts, axis=0)
    value = top + jnp.log2(jnp.sum(jnp.exp2(parts - top[None]), axis=0))
    change = base_ref[...] - (2.0 * LN2) * value
    row = lax.broadcasted_iota(jnp.int32, change.shape, 0)
    mine = jnp.sum(jnp.where(row == place_ref[0], change, 0.0), axis=0, keepdims=True)
    new_ref[...] = potential_ref[...] + 0.5 * mine
    whole = jnp.sum(jnp.sum(change * change, axis=0, keepdims=True), axis=1, keepdims=True)
    change_ref[...] = jnp.broadcast_to(whole, change_ref.shape)


def norm_kernel(count, parts_ref, out_ref):
    whole = jnp.sum(parts_ref[...], axis=0, keepdims=True)
    out_ref[...] = jnp.sqrt(whole / count + 1e-06)


def call(kernel, outs, *operands, **options):
    return pl.pallas_call(
        kernel,
        out_shape=outs,
        compiler_params=pltpu.CompilerParams(vmem_limit_bytes=VMEM),
        **options,
    )(*operands)


IN_VMEM = pl.BlockSpec(memory_space=pltpu.VMEM)
IN_SMEM = pl.BlockSpec(memory_space=pltpu.SMEM)
ANYWHERE = pl.BlockSpec(memory_space=pl.ANY)


def shape(*dims, dtype=jnp.float32):
    return jax.ShapeDtypeStruct(dims, dtype)


def per_device(points, log_point_weight, potential):
    features = points.shape[1]
    narrow = lax.axis_size("narrow")
    core = lax.axis_index("narrow") % 2
    place = lax.axis_index("wide") % MEMBERS
    own_potential = potential.reshape(1, LOCAL)
    packed = call(
        pack_kernel,
        shape(LOCAL + TAIL, features, dtype=jnp.bfloat16),
        points,
        log_point_weight.reshape(1, LOCAL),
        own_potential,
    )
    pair = lax.all_gather(
        packed,
        "narrow",
        axis=0,
        tiled=True,
        axis_index_groups=[[at, at + 1] for at in range(0, narrow, 2)],
    )
    message = call(
        spread_kernel, shape(MEMBERS, MESSAGE, features, dtype=jnp.bfloat16), pair
    )
    own = lax.all_to_all(
        message,
        AXES,
        0,
        0,
        tiled=True,
        axis_index_groups=row_groups([0]) + column_groups([1]),
    )
    other = lax.ppermute(own, "narrow", [(at, at ^ 1) for at in range(narrow)])
    sums, base = call(
        pairs_kernel,
        (shape(MEMBERS, LOCAL), shape(MEMBERS, LOCAL)),
        core.reshape(1),
        own,
        other,
        in_specs=[IN_SMEM, ANYWHERE, ANYWHERE],
        out_specs=[IN_VMEM, IN_VMEM],
        scratch_shapes=[
            pltpu.VMEM((MEMBERS, LOCAL, features), jnp.bfloat16),
            pltpu.VMEM((MEMBERS, TAIL, features), jnp.bfloat16),
            pltpu.VMEM((MEMBERS, MESSAGE, features), jnp.bfloat16),
            pltpu.VMEM((MEMBERS, 2 * LOCAL, LOCAL), jnp.float32),
            pltpu.SemaphoreType.DMA((3,)),
        ],
    )
    parts = lax.all_to_all(
        jnp.broadcast_to(sums[None], (MEMBERS, MEMBERS, LOCAL)),
        AXES,
        0,
        0,
        tiled=True,
        axis_index_groups=row_groups([0, 1]),
    )
    new_potential, change = call(
        finish_kernel,
        (shape(1, LOCAL), shape(2 * MEMBERS, LOCAL)),
        place.reshape(1),
        parts,
        base,
        own_potential,
        in_specs=[IN_SMEM, IN_VMEM, IN_VMEM, IN_VMEM],
        out_specs=[IN_VMEM, IN_VMEM],
    )
    changes = lax.all_to_all(
        change, AXES, 0, 0, tiled=True, axis_index_groups=remaining_groups()
    )
    count = LOCAL * lax.axis_size(AXES)
    norm = call(lambda a, b: norm_kernel(count, a, b), shape(1, LOCAL), changes)
    return new_potential.reshape(LOCAL), norm[0, 0]


def solution(mesh):
    in_specs = (P(AXES, None), P(AXES), P(AXES))
    out_specs = (P(AXES), P())
    return jax.shard_map(
        per_device, mesh=mesh, in_specs=in_specs, out_specs=out_specs, check_vma=False
    )
```

time: 479 us -> 109 us (0.23)
  blocking collectives: 334 us -> 64 us
  waiting for transfers between devices: 91.1 us -> 11.8 us
  matrix products: 23 us -> 0 us
  Pallas kernels: 0 us -> 20.6 us
  between operations: 15.9 us -> 0.68 us
  other arithmetic: 11.6 us -> 0 us
  starting transfers between devices: 0.04 us -> 8.86 us
    all_gather x3 -> x1, blocking collectives: 238 us -> 10.1 us  [per_device(): lax.all_gather(packed, 'narrow', axis=0, tiled=True, axis_index_groups=[[...]
    psum x1 -> x0, blocking collectives: 96.6 us -> none  [per_device(): total_change = lax.psum(jnp.sum(change * change), ('wide', 'narrow'))]
    all_gather x1 -> x0, waiting for transfers between devices: 90.5 us -> none  [per_device(): lax.all_gather(points.astype(jnp.float32), 'wide', axis=0, tiled=True)]
    all_to_all x0 -> x2, blocking collectives: none -> 53.9 us  [the longest x1 38.5 us: per_device(): lax.all_to_all(message, AXES, 0, 0, tiled=True, axis_index_groups=row_gro...]
    dot_general x16 -> x0, matrix products: 23 us -> none  [advance(): jnp.einsum('pf,qf->pq', row_points, block_points, preferred_element_type=...]
    pallas_call x0 -> x5, Pallas kernels: none -> 20.6 us  [call(): pl.pallas_call(kernel, out_shape=outs, compiler_params=pltpu.CompilerPara...]
    reduce_sum x18 -> x0, other arithmetic: 9.36 us -> none  [the longest x16 7.74 us: advance(): jnp.sum(jnp.exp(kernel_scores - highest[:, None]), axis=1)]
    all_to_all x0 -> x1, waiting for transfers between devices: none -> 7.42 us  [per_device(): lax.all_to_all(jnp.broadcast_to(sums[None], (MEMBERS, MEMBERS, LOCAL)), A...]
  transfers between devices with their start and end apart: 1 -> 2, of which waited for: 1 -> 2; matrix products, arithmetic and copies ran while one was open for 1% -> 0% of each run, Pallas kernels for 0% -> 0%
where the time goes in v1:
time: 109 us; the launch traced here: 108 us
  blocking collectives  64 us (59%)
  Pallas kernels  20.6 us (19%)
  waiting for transfers between devices  11.8 us (11%)
  starting transfers between devices  8.86 us (8%)
  local copies, waits for them, and re-layouts  2 us (2%)
    all_to_all x1, blocking collectives, per_device(): lax.all_to_all(message, AXES, 0, 0, tiled=True, axis_index_groups=row_gro...  38.5 us
    pallas_call x5, Pallas kernels, call(): pl.pallas_call(kernel, out_shape=outs, compiler_params=pltpu.CompilerPara...  20.6 us
    all_to_all x1, blocking collectives, per_device(): lax.all_to_all(change, AXES, 0, 0, tiled=True, axis_index_groups=remainin...  15.3 us
    all_gather x1, blocking collectives, per_device(): lax.all_gather(packed, 'narrow', axis=0, tiled=True, axis_index_groups=[[...  10.1 us
    all_to_all x1, waiting for transfers between devices, per_device(): lax.all_to_all(jnp.broadcast_to(sums[None], (MEMBERS, MEMBERS, LOCAL)), A...  7.42 us
    all_to_all x1, starting transfers between devices, per_device(): lax.all_to_all(jnp.broadcast_to(sums[None], (MEMBERS, MEMBERS, LOCAL)), A...  6.95 us
    ppermute x1, waiting for transfers between devices, per_device(): other = lax.ppermute(own, 'narrow', [(at, at ^ 1) for at in range(narrow)])  4.43 us
  transfers between devices with their start and end apart: 2, of which 2 were waited for; matrix products, arithmetic and copies ran while one was open for 0% of the time, Pallas kernels for 0%

profile of v1, /device:TPU:1, one launch (start us, length us, event | category | flops | bytes accessed | tf_op | source)
XLA Modules:
  0.0 108.0 jit_solution(14839540918556723432)
XLA Ops:
  0.6 1.7 %shard_map.50 = bf16[144,256]{1,0:T(8,128)(2,1)} custom-call(bf16[128,256]{1,0:T(8,128)(2,1)} %points_ref.1, f32[1,128]{1,0:T(1,128)} %bitcast.15, f32[1,128]{1,0:T(1,128)} %bitcast.13), custom_call_target="tpu_custom_call" | custom-call | tf_op jit(solution)/shard_map/pallas_call | solution.py:191
  2.3 10.1 %all_gather.3.pair_ref = bf16[288,256]{1,0:T(8,128)(2,1)} all-gather(bf16[144,256]{1,0:T(8,128)(2,1)} %shard_map.50), channel_id=1, replica_groups={{0,1},{2,3},{4,5},{6,7},{8,9},{10,11},{12,13},{14,15},{16,17},{18,19},{..., dimensions={0}, use_global_device_ids=true | all-gather | bytes 221184 | tf_op jit(solution)/shard_map/all_gather | solution.py:221
  12.4 2.4 %shard_map.51 = bf16[16,272,256]{2,1,0:T(8,128)(2,1)} custom-call(bf16[288,256]{1,0:T(8,128)(2,1)} %all_gather.3.pair_ref), custom_call_target="tpu_custom_call" | custom-call | tf_op jit(solution)/shard_map/pallas_call | solution.py:191
  14.8 38.5 %all_to_all.21.own_ref = bf16[16,272,256]{2,1,0:T(8,128)(2,1)S(1)} all-to-all(bf16[16,272,256]{2,1,0:T(8,128)(2,1)} %shard_map.51), channel_id=1, replica_groups={{0,8,16,24,32,40,48,56,64,72,80,88,96,104,112,120},{2,10,18,26,34,42,50..., dimensions={0} | all-to-all | bytes 4456448 | tf_op jit(solution)/shard_map/all_to_all | solution.py:231
  53.4 0.0 copy-start
  53.4 1.9 %collective-permute-start = (bf16[16,272,256]{2,1,0:T(8,128)(2,1)S(1)}, bf16[16,272,256]{2,1,0:T(8,128)(2,1)}, u32[]{:S(2)}, u32[]{:S(2)}) collective-permute-start(bf16[16,272,256]{2,1,0:T(8,128)(2,1)S(1)} %all_to_all.21.own_ref), channel_id=1, source_target_pairs={{0,1},{1,0},{2,3},{3,2},{4,5},{5,4},{6,7},{7,6},{8,9},{9,8},{10,11... | collective-permute-start | bytes 6684680 | tf_op jit(solution)/shard_map/ppermute | solution.py:239
  55.3 4.4 %collective-permute-done.other_ref = bf16[16,272,256]{2,1,0:T(8,128)(2,1)} collective-permute-done((bf16[16,272,256]{2,1,0:T(8,128)(2,1)S(1)}, bf16[16,272,256]{2,1,0:T(8,128)(2,1)}, u32[]{:S(2)}, u32[]{:S(2)}) %collective-permute-start) | collective-permute-done | bytes 2228256 | tf_op jit(solution)/shard_map/ppermute | solution.py:239
  59.7 0.0 copy-done
  59.7 13.6 %shard_map.52 = (f32[16,128]{1,0:T(8,128)}, f32[16,128]{1,0:T(8,128)}) custom-call(s32[1]{0:T(128)} %bitcast.1.core_ref, bf16[16,272,256]{2,1,0:T(8,128)(2,1)} %copy-done, bf16[16,272,256]{2,1,0:T(8,128)(2,1)} %collective-permute-done.other_ref), custom_call_target="tpu_custom_call" | custom-call | tf_op jit(solution)/shard_map/pallas_call | solution.py:191
  73.3 1.4 %broadcast_in_dim.2 = f32[16,16,128]{2,1,0:T(8,128)} broadcast(f32[16,128]{1,0:T(8,128)} %get-tuple-element.6), dimensions={1,2} | broadcast | bytes 139264 | tf_op jit(solution)/shard_map/broadcast_in_dim | solution.py:257
  74.7 7.0 %all-to-all-start.1 = ((f32[16,16,128]{2,1,0:T(8,128)}), f32[16,16,128]{2,1,0:T(8,128)S(1)}, u32[]{:S(2)}, u32[]{:S(2)}) async-start(f32[16,16,128]{2,1,0:T(8,128)} %broadcast_in_dim.2), calls=%async_computation.1 | async-start | bytes 262144 | tf_op jit(solution)/shard_map/all_to_all | solution.py:256
  81.7 7.4 %all-to-all-done.1.parts_ref = f32[16,16,128]{2,1,0:T(8,128)S(1)} async-done(((f32[16,16,128]{2,1,0:T(8,128)}), f32[16,16,128]{2,1,0:T(8,128)S(1)}, u32[]{:S(2)}, u32[]{:S(2)}) %all-to-all-start.1) | async-done | bytes 131104 | tf_op jit(solution)/shard_map/all_to_all | solution.py:256
  89.1 0.0 copy-start.1
  89.1 0.6 copy-done.1
  89.7 1.6 %shard_map.53 = (f32[1,128]{1,0:T(1,128)}, f32[32,128]{1,0:T(8,128)}) custom-call(s32[1]{0:T(128)} %bitcast.place_ref, f32[16,16,128]{2,1,0:T(8,128)} %copy-done.1, f32[16,128]{1,0:T(8,128)} %get-tuple-element.7.base_ref, f32[1,128]{1,0:T(1,128)} %bitcast.14), custom_call_target="tpu_custom_call" | custom-call | tf_op jit(solution)/shard_map/pallas_call | solution.py:191
  91.4 15.3 %all_to_all.22 = f32[32,1,128]{2,1,0:T(1,128)} all-to-all(f32[32,1,128]{2,1,0:T(1,128)} %bitcast.12), channel_id=1, replica_groups={{0,1,256,257,2,3,258,259,4,5,260,261,6,7,262,263,128,129,384,385,130,13..., dimensions={0} | all-to-all | bytes 32768 | tf_op jit(solution)/shard_map/all_to_all | solution.py:274
  106.7 1.2 %shard_map.54 = f32[1,128]{1,0:T(1,128)} custom-call(f32[32,128]{1,0:T(8,128)} %bitcast.11), custom_call_target="tpu_custom_call" | custom-call | tf_op jit(solution)/shard_map/pallas_call | solution.py:191
Async XLA Ops:
  53.4 6.4 %copy-start = (bf16[16,272,256]{2,1,0:T(8,128)(2,1)}, bf16[16,272,256]{2,1,0:T(8,128)(2,1)S(1)}, u32[]{:S(2)}) copy-start(bf16[16,272,256]{2,1,0:T(8,128)(2,1)S(1)} %all_to_all.21.own_ref) | copy-start | bytes 6684676
  53.4 6.4 %collective-permute-start = (bf16[16,272,256]{2,1,0:T(8,128)(2,1)S(1)}, bf16[16,272,256]{2,1,0:T(8,128)(2,1)}, u32[]{:S(2)}, u32[]{:S(2)}) collective-permute-start(bf16[16,272,256]{2,1,0:T(8,128)(2,1)S(1)} %all_to_all.21.own_ref), channel_id=1, source_target_pairs={{0,1},{1,0},{2,3},{3,2},{4,5},{5,4},{6,7},{7,6},{8,9},{9,8},{10,11... | collective-permute-start | bytes 6684680 | tf_op jit(solution)/shard_map/ppermute | solution.py:239
  74.7 14.4 %all-to-all-start.1 = ((f32[16,16,128]{2,1,0:T(8,128)}), f32[16,16,128]{2,1,0:T(8,128)S(1)}, u32[]{:S(2)}, u32[]{:S(2)}) async-start(f32[16,16,128]{2,1,0:T(8,128)} %broadcast_in_dim.2), calls=%async_computation.1 | async-start | bytes 262144 | tf_op jit(solution)/shard_map/all_to_all | solution.py:256
  89.1 0.6 copy-start.1

commit v2 on v1

--- a/solution.py
+++ b/solution.py
@@ -10,35 +10,36 @@
 LOG2E = math.log2(math.e)
 LN2 = math.log(2.0)
 AXES = ("wide", "narrow")
-SHAPE = (2, 2, 2, 8, 4, 2)
+SHAPE = (2, 4, 8, 4, 2)
 MEMBERS = 16
 LOCAL = 128
 TAIL = 16
 MESSAGE = 2 * LOCAL + TAIL
-VMEM = 56 * 1024 * 1024
-
-
-def index(z_lo, x_hi, x_lo, y, z_hi, core):
+MIB = 1024 * 1024
+PAIRS = ((0, 1), (2, 3))
+CROSS = ((1, 2), (3, 0))
+
+
+def index(x, y, z, core):
     where = 0
-    for size, at in zip(SHAPE, (z_lo, x_hi, x_lo, y, z_hi, core)):
+    for size, at in zip(SHAPE, (z % 2, x, y, z // 2, core)):
         where = where * size + at
     return where
 
 
 def row_groups(cores):
     return [
-        [index(a, b, c, y, h, core) for c in range(2) for y in range(8)]
-        for a in range(2)
-        for b in range(2)
-        for h in range(4)
+        [index(x, y, z, core) for x in pair for y in range(8)]
+        for pair in PAIRS
+        for z in range(8)
         for core in cores
     ]
 
 
 def column_groups(cores):
     return [
-        [index(a, b, c, y, h, core) for b in range(2) for h in range(4) for a in range(2)]
-        for c in range(2)
+        [index(x, y, z, core) for x in pair for z in range(8)]
+        for pair in CROSS
         for y in range(8)
         for core in cores
     ]
@@ -46,14 +47,8 @@
 
 def remaining_groups():
     return [
-        [
-            index(a, b, c, y, h, core)
-            for b in range(2)
-            for h in range(4)
-            for a in range(2)
-            for core in range(2)
-        ]
-        for c in range(2)
+        [index(x, y, z, core) for x in pair for z in range(8) for core in range(2)]
+        for pair in CROSS
         for y in range(8)
     ]
 
@@ -163,8 +158,9 @@
         top = jnp.max(highest, axis=0, keepdims=True)
         total = jnp.sum(total * jnp.exp2(highest - top), axis=0, keepdims=True)
         value = top + jnp.log2(total)
-        sum_ref[pl.ds(2 * step, 1)] = value[:, :LOCAL]
-        sum_ref[pl.ds(2 * step + 1, 1)] = value[:, LOCAL:]
+        for member in range(MEMBERS):
+            sum_ref[member, pl.ds(2 * step, 1)] = value[:, :LOCAL]
+            sum_ref[member, pl.ds(2 * step + 1, 1)] = value[:, LOCAL:]
         return unused
 
     lax.fori_loop(0, MEMBERS // 2, row_step, 0)
@@ -187,11 +183,11 @@
     out_ref[...] = jnp.sqrt(whole / count + 1e-06)
 
 
-def call(kernel, outs, *operands, **options):
+def call(kernel, outs, *operands, limit=4, **options):
     return pl.pallas_call(
         kernel,
         out_shape=outs,
-        compiler_params=pltpu.CompilerParams(vmem_limit_bytes=VMEM),
+        compiler_params=pltpu.CompilerParams(vmem_limit_bytes=limit * MIB),
         **options,
     )(*operands)
 
@@ -226,7 +222,7 @@
         axis_index_groups=[[at, at + 1] for at in range(0, narrow, 2)],
     )
     message = call(
-        spread_kernel, shape(MEMBERS, MESSAGE, features, dtype=jnp.bfloat16), pair
+        spread_kernel, shape(MEMBERS, MESSAGE, features, dtype=jnp.bfloat16), pair, limit=8
     )
     own = lax.all_to_all(
         message,
@@ -239,10 +235,11 @@
     other = lax.ppermute(own, "narrow", [(at, at ^ 1) for at in range(narrow)])
     sums, base = call(
         pairs_kernel,
-        (shape(MEMBERS, LOCAL), shape(MEMBERS, LOCAL)),
+        (shape(MEMBERS, MEMBERS, LOCAL), shape(MEMBERS, LOCAL)),
         core.reshape(1),
         own,
         other,
+        limit=24,
         in_specs=[IN_SMEM, ANYWHERE, ANYWHERE],
         out_specs=[IN_VMEM, IN_VMEM],
         scratch_shapes=[
@@ -254,7 +251,7 @@
         ],
     )
     parts = lax.all_to_all(
-        jnp.broadcast_to(sums[None], (MEMBERS, MEMBERS, LOCAL)),
+        sums,
         AXES,
         0,
         0,

time: 109 us -> 98.2 us (0.901)
  Pallas kernels: 20.6 us -> 14.3 us
  blocking collectives: 64 us -> 59.7 us
    pallas_call x5, Pallas kernels: 20.6 us -> 14.3 us  [call(): pl.pallas_call(kernel, out_shape=outs, compiler_params=pltpu.CompilerPara...]
    all_to_all x1, blocking collectives: 38.5 us -> 36 us  [per_device(): lax.all_to_all(message, AXES, 0, 0, tiled=True, axis_index_groups=row_gro...]
    all_gather x1, blocking collectives: 10.1 us -> 8.44 us  [per_device(): lax.all_gather(packed, 'narrow', axis=0, tiled=True, axis_index_groups=[[...]
    unnamed x4 -> x8, local copies, waits for them, and re-layouts: 0.65 us -> 2.15 us
    broadcast_in_dim x1 -> x0, local copies, waits for them, and re-layouts: 1.35 us -> none  [per_device(): jnp.broadcast_to(sums[None], (MEMBERS, MEMBERS, LOCAL))]
where the time goes in v2:
time: 98.2 us; the launch traced here: 97.8 us
  blocking collectives  59.7 us (61%)
  Pallas kernels  14.3 us (15%)
  waiting for transfers between devices  11.9 us (12%)
  starting transfers between devices  9.05 us (9%)
  local copies, waits for them, and re-layouts  2.15 us (2%)
    all_to_all x1, blocking collectives, per_device(): lax.all_to_all(message, AXES, 0, 0, tiled=True, axis_index_groups=row_gro...  36 us
    all_to_all x1, blocking collectives, per_device(): lax.all_to_all(change, AXES, 0, 0, tiled=True, axis_index_groups=remainin...  15.3 us
    pallas_call x5, Pallas kernels, call(): pl.pallas_call(kernel, out_shape=outs, compiler_params=pltpu.CompilerPara...  14.3 us
    all_gather x1, blocking collectives, per_device(): lax.all_gather(packed, 'narrow', axis=0, tiled=True, axis_index_groups=[[...  8.44 us
    all_to_all x1, waiting for transfers between devices, per_device(): lax.all_to_all(sums, AXES, 0, 0, tiled=True, axis_index_groups=row_groups...  7.42 us
    all_to_all x1, starting transfers between devices, per_device(): lax.all_to_all(sums, AXES, 0, 0, tiled=True, axis_index_groups=row_groups...  7.14 us
    ppermute x1, waiting for transfers between devices, per_device(): other = lax.ppermute(own, 'narrow', [(at, at ^ 1) for at in range(narrow)])  4.43 us
    unnamed x8, local copies, waits for them, and re-layouts  2.15 us
  transfers between devices with their start and end apart: 2, of which 2 were waited for; matrix products, arithmetic and copies ran while one was open for 0% of the time, Pallas kernels for 0%

profile of v2, /device:TPU:1, one launch (start us, length us, event | category | flops | bytes accessed | tf_op | source)
XLA Modules:
  0.0 97.8 jit_solution(6063633141431322219)
XLA Ops:
  0.6 0.0 copy-start
  0.6 0.8 copy-done
  1.5 0.0 copy-start.1
  1.5 0.7 copy-done.1
  2.1 0.0 copy-start.3
  2.1 0.7 copy-done.3
  2.8 0.2 shard_map.50
  2.9 8.4 %all_gather.3.pair_ref = bf16[288,256]{1,0:T(8,128)(2,1)S(1)} all-gather(bf16[144,256]{1,0:T(8,128)(2,1)S(1)} %shard_map.50), channel_id=1, replica_groups={{0,1},{2,3},{4,5},{6,7},{8,9},{10,11},{12,13},{14,15},{16,17},{18,19},{..., dimensions={0}, use_global_device_ids=true | all-gather | bytes 221184 | tf_op jit(solution)/shard_map/all_gather | solution.py:217
  11.4 0.1 shard_map.51
  11.5 36.0 %all_to_all.21.own_ref = bf16[16,272,256]{2,1,0:T(8,128)(2,1)S(1)} all-to-all(bf16[16,272,256]{2,1,0:T(8,128)(2,1)S(1)} %shard_map.51), channel_id=1, replica_groups={{0,8,16,24,32,40,48,56,64,72,80,88,96,104,112,120},{256,264,272,280,288..., dimensions={0} | all-to-all | bytes 4456448 | tf_op jit(solution)/shard_map/all_to_all | solution.py:227
  47.5 1.9 %collective-permute-start = (bf16[16,272,256]{2,1,0:T(8,128)(2,1)S(1)}, bf16[16,272,256]{2,1,0:T(8,128)(2,1)}, u32[]{:S(2)}, u32[]{:S(2)}) collective-permute-start(bf16[16,272,256]{2,1,0:T(8,128)(2,1)S(1)} %all_to_all.21.own_ref), channel_id=1, source_target_pairs={{0,1},{1,0},{2,3},{3,2},{4,5},{5,4},{6,7},{7,6},{8,9},{9,8},{10,11... | collective-permute-start | bytes 6684680 | tf_op jit(solution)/shard_map/ppermute | solution.py:235
  49.5 4.4 %collective-permute-done.other_ref = bf16[16,272,256]{2,1,0:T(8,128)(2,1)} collective-permute-done((bf16[16,272,256]{2,1,0:T(8,128)(2,1)S(1)}, bf16[16,272,256]{2,1,0:T(8,128)(2,1)}, u32[]{:S(2)}, u32[]{:S(2)}) %collective-permute-start) | collective-permute-done | bytes 2228256 | tf_op jit(solution)/shard_map/ppermute | solution.py:235
  53.9 0.0 copy-start.2
  53.9 12.9 %shard_map.52 = (f32[16,16,128]{2,1,0:T(8,128)}, f32[16,128]{1,0:T(8,128)S(1)}) custom-call(s32[1]{0:T(128)} %bitcast.1.core_ref, bf16[16,272,256]{2,1,0:T(8,128)(2,1)S(1)} %all_to_all.21.own_ref, bf16[16,272,256]{2,1,0:T(8,128)(2,1)} %collective-permute-done.other_ref), custom_call_target="tpu_custom_call" | custom-call | tf_op jit(solution)/shard_map/pallas_call | solution.py:187
  66.8 7.1 %all-to-all-start.1 = ((f32[16,16,128]{2,1,0:T(8,128)}), f32[16,16,128]{2,1,0:T(8,128)S(1)}, u32[]{:S(2)}, u32[]{:S(2)}) async-start(f32[16,16,128]{2,1,0:T(8,128)} %get-tuple-element.6), calls=%async_computation.1 | async-start | bytes 262144 | tf_op jit(solution)/shard_map/all_to_all | solution.py:253
  74.0 7.4 %all-to-all-done.1.parts_ref = f32[16,16,128]{2,1,0:T(8,128)S(1)} async-done(((f32[16,16,128]{2,1,0:T(8,128)}), f32[16,16,128]{2,1,0:T(8,128)S(1)}, u32[]{:S(2)}, u32[]{:S(2)}) %all-to-all-start.1) | async-done | bytes 131104 | tf_op jit(solution)/shard_map/all_to_all | solution.py:253
  81.4 0.0 copy-done.2
  81.4 0.6 shard_map.53
  82.0 15.3 %all_to_all.22 = f32[32,1,128]{2,1,0:T(1,128)S(1)} all-to-all(f32[32,1,128]{2,1,0:T(1,128)S(1)} %bitcast.12), channel_id=1, replica_groups={{64,65,320,321,66,67,322,323,68,69,324,325,70,71,326,327,128,129,384,38..., dimensions={0} | all-to-all | bytes 32768 | tf_op jit(solution)/shard_map/all_to_all | solution.py:271
  97.2 0.5 shard_map.54
Async XLA Ops:
  0.6 0.8 copy-start
  1.5 0.7 copy-start.1
  2.1 0.7 copy-start.3
  47.5 6.4 %collective-permute-start = (bf16[16,272,256]{2,1,0:T(8,128)(2,1)S(1)}, bf16[16,272,256]{2,1,0:T(8,128)(2,1)}, u32[]{:S(2)}, u32[]{:S(2)}) collective-permute-start(bf16[16,272,256]{2,1,0:T(8,128)(2,1)S(1)} %all_to_all.21.own_ref), channel_id=1, source_target_pairs={{0,1},{1,0},{2,3},{3,2},{4,5},{5,4},{6,7},{7,6},{8,9},{9,8},{10,11... | collective-permute-start | bytes 6684680 | tf_op jit(solution)/shard_map/ppermute | solution.py:235
  53.9 27.5 %copy-start.2 = (f32[128]{0:T(128)S(1)}, f32[128]{0:T(128)}, u32[]{:S(2)}) copy-start(f32[128]{0:T(128)} %param.5) | copy-start | bytes 1540
  66.8 14.6 %all-to-all-start.1 = ((f32[16,16,128]{2,1,0:T(8,128)}), f32[16,16,128]{2,1,0:T(8,128)S(1)}, u32[]{:S(2)}, u32[]{:S(2)}) async-start(f32[16,16,128]{2,1,0:T(8,128)} %get-tuple-element.6), calls=%async_computation.1 | async-start | bytes 262144 | tf_op jit(solution)/shard_map/all_to_all | solution.py:253

commit v3 on v2

--- a/solution.py
+++ b/solution.py
@@ -14,6 +14,7 @@
 MEMBERS = 16
 LOCAL = 128
 TAIL = 16
+TILE = 4
 MESSAGE = 2 * LOCAL + TAIL
 MIB = 1024 * 1024
 PAIRS = ((0, 1), (2, 3))
@@ -72,12 +73,13 @@
     norms = norms + lax.dot_general(ones, low, dims, preferred_element_type=jnp.float32)
     norms = norms[:1]
     potential = potential_ref[...]
-    offset = weight_ref[...] + 0.5 * potential - 0.25 * norms
-    rows = [
-        jnp.concatenate([a, b], axis=1)
-        for a, b in zip(three_terms(offset * LOG2E), three_terms(0.5 * norms - potential))
-    ]
-    half = jnp.concatenate(rows + [jnp.zeros((5, 2 * LOCAL), jnp.float32)], axis=0)
+    mass = weight_ref[...] + 0.5 * potential
+    offset = (mass - 0.25 * norms) * LOG2E
+    own_term = (mass + 0.25 * norms) * LOG2E
+    left = three_terms(offset) + three_terms(mass * LOG2E)
+    right = three_terms(0.5 * norms - potential) + three_terms(own_term)
+    rows = [jnp.concatenate(both, axis=1) for both in zip(left, right)]
+    half = jnp.concatenate(rows + [jnp.zeros((2, 2 * LOCAL), jnp.float32)], axis=0)
     out_ref[:LOCAL] = points
     out_ref[LOCAL:] = jnp.concatenate([half, half], axis=0).astype(jnp.bfloat16)
 
@@ -100,13 +102,18 @@
     core = core_ref[0]
 
     def copies(row_source, column_source):
-        return (
-            pltpu.make_async_copy(
-                row_source.at[:, pl.ds(pl.multiple_of(core * LOCAL, LOCAL), LOCAL)], rows, sems.at[0]
-            ),
-            pltpu.make_async_copy(row_source.at[:, pl.ds(2 * LOCAL, TAIL)], row_tail, sems.at[1]),
-            pltpu.make_async_copy(column_source, columns, sems.at[2]),
-        )
+        mine = pl.ds(pl.multiple_of(core * LOCAL, LOCAL), LOCAL)
+        points, tail = pl.ds(0, 2 * LOCAL), pl.ds(2 * LOCAL, TAIL)
+        plan = [
+            (row_source.at[:, tail], row_tail),
+            (column_source.at[:, tail], columns.at[:, tail]),
+            (row_source.at[:, mine], rows),
+            (column_source.at[:, points], columns.at[:, points]),
+        ]
+        return [
+            pltpu.make_async_copy(source, target, sems.at[at])
+            for at, (source, target) in enumerate(plan)
+        ]
 
     @pl.when(core == 0)
     def _():
@@ -118,37 +125,73 @@
         for copy in copies(other_ref, own_ref):
             copy.start()
 
-    for copy in copies(own_ref, other_ref):
-        copy.wait()
-
-    tails = row_tail[...].astype(jnp.float32)[:, :, LOCAL:]
-    half = lax.broadcasted_iota(jnp.int32, tails.shape, 1) // 8
-    base_ref[...] = jnp.sum(jnp.where(half == core, tails, 0.0), axis=1)
-
-    half = lax.broadcasted_iota(jnp.int32, (TAIL, LOCAL), 0) // 8
+    waits = copies(own_ref, other_ref)
+    waits[0].wait()
+    waits[1].wait()
+
+    half = lax.broadcasted_iota(jnp.int32, (MEMBERS, 8, LOCAL), 1)
+
+    def gather(tail, first):
+        pick = (half >= first) & (half < first + 3)
+        return jnp.sum(jnp.where(pick, tail, 0.0), axis=1)
+
+    tails = row_tail[...].astype(jnp.float32)
+    tails = jnp.where(core == 0, tails[:, :8], tails[:, 8:])
+    base_ref[...] = gather(tails[:, :, LOCAL:], 0)
+    own_term = gather(tails[:, :, LOCAL:], 3)
+    least = jnp.min(own_term)
+    quarter = jnp.max(own_term - gather(tails[:, :, :LOCAL], 3))
+    tails = columns[:, 2 * LOCAL :, :LOCAL].astype(jnp.float32)
+    mass = jnp.max(jnp.maximum(gather(tails[:, :8], 3), gather(tails[:, 8:], 3)))
+    near = mass + quarter - least <= 200.0
+    shift = jnp.where(near, least + 90.0, 0.0)
+
+    row = lax.broadcasted_iota(jnp.int32, (TAIL, LOCAL), 0)
     for member in range(MEMBERS):
         tail = columns[member, 2 * LOCAL :, :LOCAL]
         for side in range(2):
-            pick = jnp.where(half == side, 1.0, 0.0).astype(jnp.bfloat16)
+            pick = (row >= 8 * side) & (row < 8 * side + 3)
             offsets[member, side * LOCAL : (side + 1) * LOCAL] = lax.dot_general(
-                tail, pick, (((0,), (0,)), ((), ())), preferred_element_type=jnp.float32
-            )
-
-    scale = 0.5 * LOG2E
-
-    def row_step(step, unused):
-        mine = rows[pl.ds(2 * step, 2)].reshape(2 * LOCAL, -1)
+                tail,
+                jnp.where(pick, 1.0, 0.0).astype(jnp.bfloat16),
+                (((0,), (0,)), ((), ())),
+                preferred_element_type=jnp.float32,
+            ) - shift
+
+    waits[2].wait()
+    waits[3].wait()
+
+    def scores(member, mine):
+        inner = lax.dot_general(
+            columns[member, : 2 * LOCAL],
+            mine,
+            (((1,), (1,)), ((), ())),
+            preferred_element_type=jnp.float32,
+        )
+        score = inner * (0.5 * LOG2E) + jnp.concatenate([offsets[member]] * TILE, axis=1)
+        return score.reshape(2 * LOCAL // 8, 8, TILE * LOCAL)
+
+    def store(step, value):
+        for block in range(TILE):
+            line = value[:, block * LOCAL : (block + 1) * LOCAL]
+            for member in range(MEMBERS):
+                sum_ref[member, pl.ds(step * TILE + block, 1)] = line
+
+    def tile(step):
+        return rows[pl.ds(step * TILE, TILE)].reshape(TILE * LOCAL, -1)
+
+    def one_shift(step):
+        mine = tile(step)
+        total = jnp.zeros((8, TILE * LOCAL), jnp.float32)
+        for member in range(MEMBERS):
+            total = total + jnp.sum(jnp.exp2(scores(member, mine)), axis=0)
+        store(step, shift + jnp.log2(jnp.sum(total, axis=0, keepdims=True)))
+
+    def row_maximum(step, unused):
+        mine = tile(step)
         highest = total = None
         for member in range(MEMBERS):
-            inner = lax.dot_general(
-                columns[member, : 2 * LOCAL],
-                mine,
-                (((1,), (1,)), ((), ())),
-                preferred_element_type=jnp.float32,
-            )
-            shift = offsets[member]
-            score = inner * scale + jnp.concatenate([shift, shift], axis=1)
-            score = score.reshape(2 * LOCAL // 8, 8, 2 * LOCAL)
+            score = scores(member, mine)
             top = jnp.max(score, axis=0)
             if member:
                 top = jnp.maximum(top, highest)
@@ -157,13 +200,17 @@
             highest = top
         top = jnp.max(highest, axis=0, keepdims=True)
         total = jnp.sum(total * jnp.exp2(highest - top), axis=0, keepdims=True)
-        value = top + jnp.log2(total)
-        for member in range(MEMBERS):
-            sum_ref[member, pl.ds(2 * step, 1)] = value[:, :LOCAL]
-            sum_ref[member, pl.ds(2 * step + 1, 1)] = value[:, LOCAL:]
+        store(step, top + jnp.log2(total))
         return unused
 
-    lax.fori_loop(0, MEMBERS // 2, row_step, 0)
+    @pl.when(near)
+    def _():
+        for step in range(MEMBERS // TILE):
+            one_shift(step)
+
+    @pl.when(jnp.logical_not(near))
+    def _():
+        lax.fori_loop(0, MEMBERS // TILE, row_maximum, 0)
 
 
 def finish_kernel(place_ref, parts_ref, base_ref, potential_ref, new_ref, change_ref):
@@ -213,6 +260,7 @@
         points,
         log_point_weight.reshape(1, LOCAL),
         own_potential,
+        limit=60,
     )
     pair = lax.all_gather(
         packed,
@@ -247,7 +295,7 @@
             pltpu.VMEM((MEMBERS, TAIL, features), jnp.bfloat16),
             pltpu.VMEM((MEMBERS, MESSAGE, features), jnp.bfloat16),
             pltpu.VMEM((MEMBERS, 2 * LOCAL, LOCAL), jnp.float32),
-            pltpu.SemaphoreType.DMA((3,)),
+            pltpu.SemaphoreType.DMA((4,)),
         ],
     )
     parts = lax.all_to_all(

time: 98.2 us -> 96.5 us (0.983)
  Pallas kernels: 14.3 us -> 9.68 us
  starting transfers between devices: 9.05 us -> 12.8 us
  local copies, waits for them, and re-layouts: 2.15 us -> 0.01 us
  blocking collectives: 59.7 us -> 61.2 us
    pallas_call x5, Pallas kernels: 14.3 us -> 9.68 us  [call(): pl.pallas_call(kernel, out_shape=outs, compiler_params=pltpu.CompilerPara...]
    all_to_all x1, starting transfers between devices: 7.14 us -> 10.9 us  [per_device(): lax.all_to_all(sums, AXES, 0, 0, tiled=True, axis_index_groups=row_groups...]
    unnamed x8 -> x2, local copies, waits for them, and re-layouts: 2.15 us -> 0.01 us
    all_to_all x1, blocking collectives: 15.3 us -> 16.6 us  [per_device(): lax.all_to_all(change, AXES, 0, 0, tiled=True, axis_index_groups=remainin...]
where the time goes in v3:
time: 96.5 us; the launch traced here: 96.2 us
  blocking collectives  61.2 us (63%)
  starting transfers between devices  12.8 us (13%)
  waiting for transfers between devices  11.9 us (12%)
  Pallas kernels  9.68 us (10%)
    all_to_all x1, blocking collectives, per_device(): lax.all_to_all(message, AXES, 0, 0, tiled=True, axis_index_groups=row_gro...  36 us
    all_to_all x1, blocking collectives, per_device(): lax.all_to_all(change, AXES, 0, 0, tiled=True, axis_index_groups=remainin...  16.6 us
    all_to_all x1, starting transfers between devices, per_device(): lax.all_to_all(sums, AXES, 0, 0, tiled=True, axis_index_groups=row_groups...  10.9 us
    pallas_call x5, Pallas kernels, call(): pl.pallas_call(kernel, out_shape=outs, compiler_params=pltpu.CompilerPara...  9.68 us
    all_gather x1, blocking collectives, per_device(): lax.all_gather(packed, 'narrow', axis=0, tiled=True, axis_index_groups=[[...  8.64 us
    all_to_all x1, waiting for transfers between devices, per_device(): lax.all_to_all(sums, AXES, 0, 0, tiled=True, axis_index_groups=row_groups...  7.42 us
    ppermute x1, waiting for transfers between devices, per_device(): other = lax.ppermute(own, 'narrow', [(at, at ^ 1) for at in range(narrow)])  4.43 us
  transfers between devices with their start and end apart: 2, of which 2 were waited for; matrix products, arithmetic and copies ran while one was open for 0% of the time, Pallas kernels for 0%

profile of v3, /device:TPU:1, one launch (start us, length us, event | category | flops | bytes accessed | tf_op | source)
XLA Modules:
  0.0 96.2 jit_solution(598007986012510390)
XLA Ops:
  0.6 1.7 %shard_map.50 = bf16[144,256]{1,0:T(8,128)(2,1)} custom-call(bf16[128,256]{1,0:T(8,128)(2,1)} %points_ref.1, f32[1,128]{1,0:T(1,128)} %bitcast.15, f32[1,128]{1,0:T(1,128)} %bitcast.13), custom_call_target="tpu_custom_call" | custom-call | tf_op jit(solution)/shard_map/pallas_call | solution.py:234
  2.3 8.6 %all_gather.3.pair_ref = bf16[288,256]{1,0:T(8,128)(2,1)S(1)} all-gather(bf16[144,256]{1,0:T(8,128)(2,1)} %shard_map.50), channel_id=1, replica_groups={{0,1},{2,3},{4,5},{6,7},{8,9},{10,11},{12,13},{14,15},{16,17},{18,19},{..., dimensions={0}, use_global_device_ids=true | all-gather | bytes 221184 | tf_op jit(solution)/shard_map/all_gather | solution.py:265
  10.9 0.1 shard_map.51
  11.1 36.0 %all_to_all.21.own_ref = bf16[16,272,256]{2,1,0:T(8,128)(2,1)S(1)} all-to-all(bf16[16,272,256]{2,1,0:T(8,128)(2,1)S(1)} %shard_map.51), channel_id=1, replica_groups={{0,8,16,24,32,40,48,56,64,72,80,88,96,104,112,120},{256,264,272,280,288..., dimensions={0} | all-to-all | bytes 4456448 | tf_op jit(solution)/shard_map/all_to_all | solution.py:275
  47.1 1.9 %collective-permute-start = (bf16[16,272,256]{2,1,0:T(8,128)(2,1)S(1)}, bf16[16,272,256]{2,1,0:T(8,128)(2,1)}, u32[]{:S(2)}, u32[]{:S(2)}) collective-permute-start(bf16[16,272,256]{2,1,0:T(8,128)(2,1)S(1)} %all_to_all.21.own_ref), channel_id=1, source_target_pairs={{0,1},{1,0},{2,3},{3,2},{4,5},{5,4},{6,7},{7,6},{8,9},{9,8},{10,11... | collective-permute-start | bytes 6684680 | tf_op jit(solution)/shard_map/ppermute | solution.py:283
  49.0 4.4 %collective-permute-done.other_ref = bf16[16,272,256]{2,1,0:T(8,128)(2,1)} collective-permute-done((bf16[16,272,256]{2,1,0:T(8,128)(2,1)S(1)}, bf16[16,272,256]{2,1,0:T(8,128)(2,1)}, u32[]{:S(2)}, u32[]{:S(2)}) %collective-permute-start) | collective-permute-done | bytes 2228256 | tf_op jit(solution)/shard_map/ppermute | solution.py:283
  53.4 0.0 copy-start
  53.4 6.8 %shard_map.52 = (f32[16,16,128]{2,1,0:T(8,128)}, f32[16,128]{1,0:T(8,128)S(1)}) custom-call(s32[1]{0:T(128)} %bitcast.1.core_ref, bf16[16,272,256]{2,1,0:T(8,128)(2,1)S(1)} %all_to_all.21.own_ref, bf16[16,272,256]{2,1,0:T(8,128)(2,1)} %collective-permute-done.other_ref), custom_call_target="tpu_custom_call" | custom-call | tf_op jit(solution)/shard_map/pallas_call | solution.py:234
  60.2 10.9 %all-to-all-start.1 = ((f32[16,16,128]{2,1,0:T(8,128)}), f32[16,16,128]{2,1,0:T(8,128)S(1)}, u32[]{:S(2)}, u32[]{:S(2)}) async-start(f32[16,16,128]{2,1,0:T(8,128)} %get-tuple-element.6), calls=%async_computation.1 | async-start | bytes 262144 | tf_op jit(solution)/shard_map/all_to_all | solution.py:301
  71.1 7.4 %all-to-all-done.1.parts_ref = f32[16,16,128]{2,1,0:T(8,128)S(1)} async-done(((f32[16,16,128]{2,1,0:T(8,128)}), f32[16,16,128]{2,1,0:T(8,128)S(1)}, u32[]{:S(2)}, u32[]{:S(2)}) %all-to-all-start.1) | async-done | bytes 131104 | tf_op jit(solution)/shard_map/all_to_all | solution.py:301
  78.5 0.0 copy-done
  78.5 0.6 shard_map.53
  79.1 16.6 %all_to_all.22 = f32[32,1,128]{2,1,0:T(1,128)S(1)} all-to-all(f32[32,1,128]{2,1,0:T(1,128)S(1)} %bitcast.12), channel_id=1, replica_groups={{64,65,320,321,66,67,322,323,68,69,324,325,70,71,326,327,128,129,384,38..., dimensions={0} | all-to-all | bytes 32768 | tf_op jit(solution)/shard_map/all_to_all | solution.py:319
  95.7 0.5 shard_map.54
Async XLA Ops:
  47.1 6.4 %collective-permute-start = (bf16[16,272,256]{2,1,0:T(8,128)(2,1)S(1)}, bf16[16,272,256]{2,1,0:T(8,128)(2,1)}, u32[]{:S(2)}, u32[]{:S(2)}) collective-permute-start(bf16[16,272,256]{2,1,0:T(8,128)(2,1)S(1)} %all_to_all.21.own_ref), channel_id=1, source_target_pairs={{0,1},{1,0},{2,3},{3,2},{4,5},{5,4},{6,7},{7,6},{8,9},{9,8},{10,11... | collective-permute-start | bytes 6684680 | tf_op jit(solution)/shard_map/ppermute | solution.py:283
  53.4 25.1 %copy-start = (f32[128]{0:T(128)S(1)}, f32[128]{0:T(128)}, u32[]{:S(2)}) copy-start(f32[128]{0:T(128)} %param.5) | copy-start | bytes 1540
  60.2 18.3 %all-to-all-start.1 = ((f32[16,16,128]{2,1,0:T(8,128)}), f32[16,16,128]{2,1,0:T(8,128)S(1)}, u32[]{:S(2)}, u32[]{:S(2)}) async-start(f32[16,16,128]{2,1,0:T(8,128)} %get-tuple-element.6), calls=%async_computation.1 | async-start | bytes 262144 | tf_op jit(solution)/shard_map/all_to_all | solution.py:301

commit v4 on v3

--- a/solution.py
+++ b/solution.py
@@ -97,9 +97,9 @@
 
 
 def pairs_kernel(
-    core_ref, own_ref, other_ref, sum_ref, base_ref, rows, row_tail, columns, offsets, sems
+    own_ref, other_ref, sum_ref, base_ref, rows, row_tail, columns, offsets, sems
 ):
-    core = core_ref[0]
+    core = lax.axis_index("narrow") & 1
 
     def copies(row_source, column_source):
         mine = pl.ds(pl.multiple_of(core * LOCAL, LOCAL), LOCAL)
@@ -213,13 +213,13 @@
         lax.fori_loop(0, MEMBERS // TILE, row_maximum, 0)
 
 
-def finish_kernel(place_ref, parts_ref, base_ref, potential_ref, new_ref, change_ref):
+def finish_kernel(parts_ref, base_ref, potential_ref, new_ref, change_ref):
     parts = parts_ref[...]
     top = jnp.max(parts, axis=0)
     value = top + jnp.log2(jnp.sum(jnp.exp2(parts - top[None]), axis=0))
     change = base_ref[...] - (2.0 * LN2) * value
     row = lax.broadcasted_iota(jnp.int32, change.shape, 0)
-    mine = jnp.sum(jnp.where(row == place_ref[0], change, 0.0), axis=0, keepdims=True)
+    mine = jnp.sum(jnp.where(row == lax.axis_index("wide") & (MEMBERS - 1), change, 0.0), axis=0, keepdims=True)
     new_ref[...] = potential_ref[...] + 0.5 * mine
     whole = jnp.sum(jnp.sum(change * change, axis=0, keepdims=True), axis=1, keepdims=True)
     change_ref[...] = jnp.broadcast_to(whole, change_ref.shape)
@@ -240,7 +240,6 @@
 
 
 IN_VMEM = pl.BlockSpec(memory_space=pltpu.VMEM)
-IN_SMEM = pl.BlockSpec(memory_space=pltpu.SMEM)
 ANYWHERE = pl.BlockSpec(memory_space=pl.ANY)
 
 
@@ -251,8 +250,6 @@
 def per_device(points, log_point_weight, potential):
     features = points.shape[1]
     narrow = lax.axis_size("narrow")
-    core = lax.axis_index("narrow") % 2
-    place = lax.axis_index("wide") % MEMBERS
     own_potential = potential.reshape(1, LOCAL)
     packed = call(
         pack_kernel,
@@ -284,11 +281,10 @@
     sums, base = call(
         pairs_kernel,
         (shape(MEMBERS, MEMBERS, LOCAL), shape(MEMBERS, LOCAL)),
-        core.reshape(1),
         own,
         other,
-        limit=24,
-        in_specs=[IN_SMEM, ANYWHERE, ANYWHERE],
+        limit=16,
+        in_specs=[ANYWHERE, ANYWHERE],
         out_specs=[IN_VMEM, IN_VMEM],
         scratch_shapes=[
             pltpu.VMEM((MEMBERS, LOCAL, features), jnp.bfloat16),
@@ -309,11 +305,10 @@
     new_potential, change = call(
         finish_kernel,
         (shape(1, LOCAL), shape(2 * MEMBERS, LOCAL)),
-        place.reshape(1),
         parts,
         base,
         own_potential,
-        in_specs=[IN_SMEM, IN_VMEM, IN_VMEM, IN_VMEM],
+        in_specs=[IN_VMEM, IN_VMEM, IN_VMEM],
         out_specs=[IN_VMEM, IN_VMEM],
     )
     changes = lax.all_to_all(

time: 96.5 us -> 94.6 us (0.980)
  blocking collectives: 61.2 us -> 79 us
  starting transfers between devices: 12.8 us -> 2.04 us
  waiting for transfers between devices: 11.9 us -> 4.31 us
  Pallas kernels: 9.68 us -> 8.36 us
    all_to_all x0 -> x1, blocking collectives: none -> 18.9 us  [per_device(): lax.all_to_all(sums, AXES, 0, 0, tiled=True, axis_index_groups=row_groups...]
    all_to_all x1 -> x0, starting transfers between devices: 10.9 us -> none  [per_device(): lax.all_to_all(sums, AXES, 0, 0, tiled=True, axis_index_groups=row_groups...]
    all_to_all x1 -> x0, waiting for transfers between devices: 7.42 us -> none  [per_device(): lax.all_to_all(sums, AXES, 0, 0, tiled=True, axis_index_groups=row_groups...]
    pallas_call x5, Pallas kernels: 9.68 us -> 8.36 us  [call(): pl.pallas_call(kernel, out_shape=outs, compiler_params=pltpu.CompilerPara...]
    all_to_all x1, blocking collectives: 16.6 us -> 15.5 us  [per_device(): lax.all_to_all(change, AXES, 0, 0, tiled=True, axis_index_groups=remainin...]
  transfers between devices with their start and end apart: 2 -> 1, of which waited for: 2 -> 1; matrix products, arithmetic and copies ran while one was open for 0% -> 0% of each run, Pallas kernels for 0% -> 0%
where the time goes in v4:
time: 94.6 us; the launch traced here: 94.4 us
  blocking collectives  79 us (84%)
  Pallas kernels  8.36 us (9%)
  waiting for transfers between devices  4.31 us (5%)
  starting transfers between devices  2.04 us (2%)
    all_to_all x1, blocking collectives, per_device(): lax.all_to_all(message, AXES, 0, 0, tiled=True, axis_index_groups=row_gro...  36 us
    all_to_all x1, blocking collectives, per_device(): lax.all_to_all(sums, AXES, 0, 0, tiled=True, axis_index_groups=row_groups...  18.9 us
    all_to_all x1, blocking collectives, per_device(): lax.all_to_all(change, AXES, 0, 0, tiled=True, axis_index_groups=remainin...  15.5 us
    all_gather x1, blocking collectives, per_device(): lax.all_gather(packed, 'narrow', axis=0, tiled=True, axis_index_groups=[[...  8.64 us
    pallas_call x5, Pallas kernels, call(): pl.pallas_call(kernel, out_shape=outs, compiler_params=pltpu.CompilerPara...  8.36 us
    ppermute x1, waiting for transfers between devices, per_device(): other = lax.ppermute(own, 'narrow', [(at, at ^ 1) for at in range(narrow)])  4.31 us
    ppermute x1, starting transfers between devices, per_device(): other = lax.ppermute(own, 'narrow', [(at, at ^ 1) for at in range(narrow)])  2.04 us
  transfers between devices with their start and end apart: 1, of which 1 were waited for; matrix products, arithmetic and copies ran while one was open for 0% of the time, Pallas kernels for 0%

profile of v4, /device:TPU:1, one launch (start us, length us, event | category | flops | bytes accessed | tf_op | source)
XLA Modules:
  0.0 94.4 jit_solution(16304762522614942460)
XLA Ops:
  0.6 1.7 %shard_map.50 = bf16[144,256]{1,0:T(8,128)(2,1)} custom-call(bf16[128,256]{1,0:T(8,128)(2,1)} %points_ref.1, f32[1,128]{1,0:T(1,128)} %bitcast.13, f32[1,128]{1,0:T(1,128)} %bitcast.11), custom_call_target="tpu_custom_call" | custom-call | tf_op jit(solution)/shard_map/pallas_call | solution.py:234
  2.3 8.6 %all_gather.3.pair_ref = bf16[288,256]{1,0:T(8,128)(2,1)S(1)} all-gather(bf16[144,256]{1,0:T(8,128)(2,1)} %shard_map.50), channel_id=1, replica_groups={{0,1},{2,3},{4,5},{6,7},{8,9},{10,11},{12,13},{14,15},{16,17},{18,19},{..., dimensions={0}, use_global_device_ids=true | all-gather | bytes 221184 | tf_op jit(solution)/shard_map/all_gather | solution.py:262
  10.9 0.1 shard_map.51
  11.1 36.0 %all_to_all.21.own_ref = bf16[16,272,256]{2,1,0:T(8,128)(2,1)S(1)} all-to-all(bf16[16,272,256]{2,1,0:T(8,128)(2,1)S(1)} %shard_map.51), channel_id=1, replica_groups={{0,8,16,24,32,40,48,56,64,72,80,88,96,104,112,120},{256,264,272,280,288..., dimensions={0} | all-to-all | bytes 4456448 | tf_op jit(solution)/shard_map/all_to_all | solution.py:272
  47.1 0.0 copy-start
  47.1 2.0 %collective-permute-start = (bf16[16,272,256]{2,1,0:T(8,128)(2,1)S(1)}, bf16[16,272,256]{2,1,0:T(8,128)(2,1)S(1)}, u32[]{:S(2)}, u32[]{:S(2)}) collective-permute-start(bf16[16,272,256]{2,1,0:T(8,128)(2,1)S(1)} %all_to_all.21.own_ref), channel_id=1, source_target_pairs={{0,1},{1,0},{2,3},{3,2},{4,5},{5,4},{6,7},{7,6},{8,9},{9,8},{10,11... | collective-permute-start | bytes 6684680 | tf_op jit(solution)/shard_map/ppermute | solution.py:280
  49.1 4.3 %collective-permute-done.other_ref = bf16[16,272,256]{2,1,0:T(8,128)(2,1)S(1)} collective-permute-done((bf16[16,272,256]{2,1,0:T(8,128)(2,1)S(1)}, bf16[16,272,256]{2,1,0:T(8,128)(2,1)S(1)}, u32[]{:S(2)}, u32[]{:S(2)}) %collective-permute-start) | collective-permute-done | bytes 2228256 | tf_op jit(solution)/shard_map/ppermute | solution.py:280
  53.4 5.5 %shard_map.52 = (f32[16,16,128]{2,1,0:T(8,128)S(1)}, f32[16,128]{1,0:T(8,128)S(1)}) custom-call(bf16[16,272,256]{2,1,0:T(8,128)(2,1)S(1)} %all_to_all.21.own_ref, bf16[16,272,256]{2,1,0:T(8,128)(2,1)S(1)} %collective-permute-done.other_ref), custom_call_target="tpu_custom_call" | custom-call | tf_op jit(solution)/shard_map/pallas_call | solution.py:234
  58.9 18.9 %all_to_all.22.parts_ref = f32[16,16,128]{2,1,0:T(8,128)S(1)} all-to-all(f32[16,16,128]{2,1,0:T(8,128)S(1)} %get-tuple-element.6), channel_id=1, replica_groups={{0,8,16,24,32,40,48,56,64,72,80,88,96,104,112,120},{1,9,17,25,33,41,49,..., dimensions={0} | all-to-all | bytes 262144 | tf_op jit(solution)/shard_map/all_to_all | solution.py:297
  77.8 0.0 copy-done
  77.8 0.6 shard_map.53
  78.3 15.5 %all_to_all.23 = f32[32,1,128]{2,1,0:T(1,128)S(1)} all-to-all(f32[32,1,128]{2,1,0:T(1,128)S(1)} %bitcast.10), channel_id=1, replica_groups={{64,65,320,321,66,67,322,323,68,69,324,325,70,71,326,327,128,129,384,38..., dimensions={0} | all-to-all | bytes 32768 | tf_op jit(solution)/shard_map/all_to_all | solution.py:314
  93.8 0.5 shard_map.54
Async XLA Ops:
  47.1 30.7 %copy-start = (f32[128]{0:T(128)S(1)}, f32[128]{0:T(128)}, u32[]{:S(2)}) copy-start(f32[128]{0:T(128)} %param.5) | copy-start | bytes 1540
  47.1 6.4 %collective-permute-start = (bf16[16,272,256]{2,1,0:T(8,128)(2,1)S(1)}, bf16[16,272,256]{2,1,0:T(8,128)(2,1)S(1)}, u32[]{:S(2)}, u32[]{:S(2)}) collective-permute-start(bf16[16,272,256]{2,1,0:T(8,128)(2,1)S(1)} %all_to_all.21.own_ref), channel_id=1, source_target_pairs={{0,1},{1,0},{2,3},{3,2},{4,5},{5,4},{6,7},{7,6},{8,9},{9,8},{10,11... | collective-permute-start | bytes 6684680 | tf_op jit(solution)/shard_map/ppermute | solution.py:280

commit v5 on v4

--- a/solution.py
+++ b/solution.py
@@ -1,3 +1,4 @@
+import functools
 import math
 
 import jax
@@ -96,121 +97,115 @@
         out_ref[member, 2 * LOCAL :] = tail
 
 
-def pairs_kernel(
-    own_ref, other_ref, sum_ref, base_ref, rows, row_tail, columns, offsets, sems
-):
-    core = lax.axis_index("narrow") & 1
-
-    def copies(row_source, column_source):
-        mine = pl.ds(pl.multiple_of(core * LOCAL, LOCAL), LOCAL)
-        points, tail = pl.ds(0, 2 * LOCAL), pl.ds(2 * LOCAL, TAIL)
-        plan = [
-            (row_source.at[:, tail], row_tail),
-            (column_source.at[:, tail], columns.at[:, tail]),
-            (row_source.at[:, mine], rows),
-            (column_source.at[:, points], columns.at[:, points]),
-        ]
-        return [
-            pltpu.make_async_copy(source, target, sems.at[at])
-            for at, (source, target) in enumerate(plan)
-        ]
-
-    @pl.when(core == 0)
-    def _():
-        for copy in copies(own_ref, other_ref):
-            copy.start()
-
-    @pl.when(core == 1)
-    def _():
-        for copy in copies(other_ref, own_ref):
-            copy.start()
-
-    waits = copies(own_ref, other_ref)
-    waits[0].wait()
-    waits[1].wait()
-
-    half = lax.broadcasted_iota(jnp.int32, (MEMBERS, 8, LOCAL), 1)
+def log_sums(row_ref, column_ref, core, offsets):
+    line = lax.broadcasted_iota(jnp.int32, (1, 8, LOCAL), 1)
 
     def gather(tail, first):
-        pick = (half >= first) & (half < first + 3)
+        pick = (line >= first) & (line < first + 3)
         return jnp.sum(jnp.where(pick, tail, 0.0), axis=1)
 
-    tails = row_tail[...].astype(jnp.float32)
-    tails = jnp.where(core == 0, tails[:, :8], tails[:, 8:])
-    base_ref[...] = gather(tails[:, :, LOCAL:], 0)
+    own = slice(2 * LOCAL, MESSAGE)
+    tails = row_ref[:, own].astype(jnp.float32)[:, 8 * core : 8 * core + 8]
+    base = gather(tails[:, :, LOCAL:], 0)
     own_term = gather(tails[:, :, LOCAL:], 3)
     least = jnp.min(own_term)
     quarter = jnp.max(own_term - gather(tails[:, :, :LOCAL], 3))
-    tails = columns[:, 2 * LOCAL :, :LOCAL].astype(jnp.float32)
+    tails = column_ref[:, own, :LOCAL].astype(jnp.float32)
     mass = jnp.max(jnp.maximum(gather(tails[:, :8], 3), gather(tails[:, 8:], 3)))
     near = mass + quarter - least <= 200.0
     shift = jnp.where(near, least + 90.0, 0.0)
 
     row = lax.broadcasted_iota(jnp.int32, (TAIL, LOCAL), 0)
-    for member in range(MEMBERS):
-        tail = columns[member, 2 * LOCAL :, :LOCAL]
+    columns = column_ref.shape[0]
+    for block in range(columns):
         for side in range(2):
             pick = (row >= 8 * side) & (row < 8 * side + 3)
-            offsets[member, side * LOCAL : (side + 1) * LOCAL] = lax.dot_general(
-                tail,
+            offsets[block, side * LOCAL : (side + 1) * LOCAL] = lax.dot_general(
+                column_ref[block, own, :LOCAL],
                 jnp.where(pick, 1.0, 0.0).astype(jnp.bfloat16),
                 (((0,), (0,)), ((), ())),
                 preferred_element_type=jnp.float32,
             ) - shift
 
-    waits[2].wait()
-    waits[3].wait()
-
-    def scores(member, mine):
+    def scores(block, mine):
         inner = lax.dot_general(
-            columns[member, : 2 * LOCAL],
+            column_ref[block, : 2 * LOCAL],
             mine,
             (((1,), (1,)), ((), ())),
             preferred_element_type=jnp.float32,
         )
-        score = inner * (0.5 * LOG2E) + jnp.concatenate([offsets[member]] * TILE, axis=1)
+        score = inner * (0.5 * LOG2E) + jnp.concatenate([offsets[block]] * TILE, axis=1)
         return score.reshape(2 * LOCAL // 8, 8, TILE * LOCAL)
 
-    def store(step, value):
-        for block in range(TILE):
-            line = value[:, block * LOCAL : (block + 1) * LOCAL]
-            for member in range(MEMBERS):
-                sum_ref[member, pl.ds(step * TILE + block, 1)] = line
-
-    def tile(step):
-        return rows[pl.ds(step * TILE, TILE)].reshape(TILE * LOCAL, -1)
-
-    def one_shift(step):
-        mine = tile(step)
+    def one_shift(mine):
         total = jnp.zeros((8, TILE * LOCAL), jnp.float32)
-        for member in range(MEMBERS):
-            total = total + jnp.sum(jnp.exp2(scores(member, mine)), axis=0)
-        store(step, shift + jnp.log2(jnp.sum(total, axis=0, keepdims=True)))
-
-    def row_maximum(step, unused):
-        mine = tile(step)
-        highest = total = None
-        for member in range(MEMBERS):
-            score = scores(member, mine)
-            top = jnp.max(score, axis=0)
-            if member:
-                top = jnp.maximum(top, highest)
-            part = jnp.sum(jnp.exp2(score - top[None]), axis=0)
-            total = part if member == 0 else part + total * jnp.exp2(highest - top)
-            highest = top
+        for block in range(columns):
+            total = total + jnp.sum(jnp.exp2(scores(block, mine)), axis=0)
+        total = jnp.maximum(jnp.sum(total, axis=0, keepdims=True), 2.0**-126)
+        return shift + jnp.log2(total)
+
+    def row_maximum(mine):
+        def step(block, carry):
+            highest, total = carry
+            score = scores(block, mine)
+            top = jnp.maximum(highest, jnp.max(score, axis=0))
+            total = total * jnp.exp2(highest - top) + jnp.sum(jnp.exp2(score - top[None]), axis=0)
+            return top, total
+
+        start = jnp.full((8, TILE * LOCAL), -1e30, jnp.float32)
+        highest, total = lax.fori_loop(0, columns, step, (start, jnp.zeros_like(start)))
         top = jnp.max(highest, axis=0, keepdims=True)
         total = jnp.sum(total * jnp.exp2(highest - top), axis=0, keepdims=True)
-        store(step, top + jnp.log2(total))
-        return unused
-
-    @pl.when(near)
+        return top + jnp.log2(total)
+
+    def run(method):
+        lines = []
+        for step in range(0, row_ref.shape[0], TILE):
+            mine = row_ref[step : step + TILE, core * LOCAL : (core + 1) * LOCAL]
+            value = method(mine.reshape(TILE * LOCAL, -1))
+            lines += [value[:, at * LOCAL : (at + 1) * LOCAL] for at in range(TILE)]
+        return jnp.concatenate(lines, axis=0)
+
+    return lax.cond(near, lambda: run(one_shift), lambda: run(row_maximum)), base
+
+
+def pairs_kernel(final, own_ref, part_ref, *refs):
+    if final:
+        sum_before, base_before, sum_ref, base_ref, offsets = refs
+    else:
+        sum_ref, base_ref, offsets = refs
+    where = lax.axis_index("narrow") & 1
+    half = MEMBERS // 2
+
+    def store(value, base):
+        base_ref[...] = base
+        if not final:
+            sum_ref[...] = value
+            return
+        before = sum_before[...]
+        top = jnp.maximum(before, value)
+        value = top + jnp.log2(jnp.exp2(before - top) + jnp.exp2(value - top))
+        for member in range(MEMBERS):
+            sum_ref[member] = value
+
+    @pl.when(where == 0)
     def _():
-        for step in range(MEMBERS // TILE):
-            one_shift(step)
-
-    @pl.when(jnp.logical_not(near))
+        store(*log_sums(own_ref, part_ref, 0, offsets))
+
+    @pl.when(where == 1)
     def _():
-        lax.fori_loop(0, MEMBERS // TILE, row_maximum, 0)
+        value, base = log_sums(part_ref, own_ref, 1, offsets)
+        missing = jnp.full(value.shape, -1e30, jnp.float32)
+        if final:
+            store(
+                jnp.concatenate([missing, value], axis=0),
+                jnp.concatenate([base_before[:half], base], axis=0),
+            )
+        else:
+            store(
+                jnp.concatenate([value, missing], axis=0),
+                jnp.concatenate([base, base], axis=0),
+            )
 
 
 def finish_kernel(parts_ref, base_ref, potential_ref, new_ref, change_ref):
@@ -240,7 +235,6 @@
 
 
 IN_VMEM = pl.BlockSpec(memory_space=pltpu.VMEM)
-ANYWHERE = pl.BlockSpec(memory_space=pl.ANY)
 
 
 def shape(*dims, dtype=jnp.float32):
@@ -277,22 +271,26 @@
         tiled=True,
         axis_index_groups=row_groups([0]) + column_groups([1]),
     )
-    other = lax.ppermute(own, "narrow", [(at, at ^ 1) for at in range(narrow)])
+    other_core = [(at, at ^ 1) for at in range(narrow)]
+    halves = [lax.ppermute(part, "narrow", other_core) for part in jnp.split(own, 2)]
+    offsets = [pltpu.VMEM((MEMBERS, 2 * LOCAL, LOCAL), jnp.float32)]
+    lines = shape(MEMBERS, LOCAL)
+    before = call(
+        functools.partial(pairs_kernel, False),
+        (lines, lines),
+        own,
+        halves[0],
+        limit=10,
+        scratch_shapes=offsets,
+    )
     sums, base = call(
-        pairs_kernel,
-        (shape(MEMBERS, MEMBERS, LOCAL), shape(MEMBERS, LOCAL)),
+        functools.partial(pairs_kernel, True),
+        (shape(MEMBERS, MEMBERS, LOCAL), lines),
         own,
-        other,
-        limit=16,
-        in_specs=[ANYWHERE, ANYWHERE],
-        out_specs=[IN_VMEM, IN_VMEM],
-        scratch_shapes=[
-            pltpu.VMEM((MEMBERS, LOCAL, features), jnp.bfloat16),
-            pltpu.VMEM((MEMBERS, TAIL, features), jnp.bfloat16),
-            pltpu.VMEM((MEMBERS, MESSAGE, features), jnp.bfloat16),
-            pltpu.VMEM((MEMBERS, 2 * LOCAL, LOCAL), jnp.float32),
-            pltpu.SemaphoreType.DMA((4,)),
-        ],
+        halves[1],
+        *before,
+        limit=10,
+        scratch_shapes=offsets,
     )
     parts = lax.all_to_all(
         sums,

time: 94.6 us -> 107 us (1.13)
  blocking collectives: 79 us -> 92 us
  waiting for transfers between devices: 4.31 us -> 0.31 us
  starting transfers between devices: 2.04 us -> 4.33 us
    all_to_all x1, blocking collectives: 18.9 us -> 32.8 us  [per_device(): lax.all_to_all(sums, AXES, 0, 0, tiled=True, axis_index_groups=row_groups...]
    ppermute x1 -> x2, waiting for transfers between devices: 4.31 us -> 0.31 us  [per_device(): lax.ppermute(part, 'narrow', other_core)]
    ppermute x1 -> x2, starting transfers between devices: 2.04 us -> 4.33 us  [per_device(): lax.ppermute(part, 'narrow', other_core)]
    pallas_call x5 -> x6, Pallas kernels: 8.36 us -> 9.24 us  [call(): pl.pallas_call(kernel, out_shape=outs, compiler_params=pltpu.CompilerPara...]
  transfers between devices with their start and end apart: 1 -> 2, of which waited for: 1 -> 1; matrix products, arithmetic and copies ran while one was open for 0% -> 0% of each run, Pallas kernels for 0% -> 3%
where the time goes in v5:
time: 107 us
  blocking collectives  92 us (86%)
  Pallas kernels  9.24 us (9%)
  starting transfers between devices  4.33 us (4%)
    all_to_all x1, blocking collectives, per_device(): lax.all_to_all(message, AXES, 0, 0, tiled=True, axis_index_groups=row_gro...  36 us
    all_to_all x1, blocking collectives, per_device(): lax.all_to_all(sums, AXES, 0, 0, tiled=True, axis_index_groups=row_groups...  32.8 us
    all_to_all x1, blocking collectives, per_device(): lax.all_to_all(change, AXES, 0, 0, tiled=True, axis_index_groups=remainin...  14.6 us
    pallas_call x6, Pallas kernels, call(): pl.pallas_call(kernel, out_shape=outs, compiler_params=pltpu.CompilerPara...  9.24 us
    all_gather x1, blocking collectives, per_device(): lax.all_gather(packed, 'narrow', axis=0, tiled=True, axis_index_groups=[[...  8.64 us
    ppermute x2, starting transfers between devices, per_device(): lax.ppermute(part, 'narrow', other_core)  4.33 us
  transfers between devices with their start and end apart: 2, of which 1 were waited for; matrix products, arithmetic and copies ran while one was open for 0% of the time, Pallas kernels for 3%

profile of v5, /device:TPU:1, one launch (start us, length us, event | category | flops | bytes accessed | tf_op | source)
XLA Modules:
  0.0 106.7 jit_solution(17177743408783319549)
XLA Ops:
  0.6 1.7 %shard_map.50 = bf16[144,256]{1,0:T(8,128)(2,1)} custom-call(bf16[128,256]{1,0:T(8,128)(2,1)} %points_ref.1, f32[1,128]{1,0:T(1,128)} %bitcast.13, f32[1,128]{1,0:T(1,128)} %bitcast.11), custom_call_target="tpu_custom_call" | custom-call | tf_op jit(solution)/shard_map/pallas_call | solution.py:229
  2.3 8.6 %all_gather.3.pair_ref = bf16[288,256]{1,0:T(8,128)(2,1)S(1)} all-gather(bf16[144,256]{1,0:T(8,128)(2,1)} %shard_map.50), channel_id=1, replica_groups={{0,1},{2,3},{4,5},{6,7},{8,9},{10,11},{12,13},{14,15},{16,17},{18,19},{..., dimensions={0}, use_global_device_ids=true | all-gather | bytes 221184 | tf_op jit(solution)/shard_map/all_gather | solution.py:256
  10.9 0.1 shard_map.51
  11.1 36.0 %all_to_all.21.own_ref = bf16[16,272,256]{2,1,0:T(8,128)(2,1)S(1)} all-to-all(bf16[16,272,256]{2,1,0:T(8,128)(2,1)S(1)} %shard_map.51), channel_id=1, replica_groups={{0,8,16,24,32,40,48,56,64,72,80,88,96,104,112,120},{256,264,272,280,288..., dimensions={0} | all-to-all | bytes 4456448 | tf_op jit(solution)/shard_map/all_to_all | solution.py:266
  47.1 0.1 fusion
  47.2 1.9 %collective-permute-start.1 = (bf16[8,272,256]{2,1,0:T(8,128)(2,1)S(1)}, bf16[8,272,256]{2,1,0:T(8,128)(2,1)S(1)}, u32[]{:S(2)}, u32[]{:S(2)}) collective-permute-start(bf16[8,272,256]{2,1,0:T(8,128)(2,1)S(1)} %get-tuple-element.14), channel_id=1, source_target_pairs={{0,1},{1,0},{2,3},{3,2},{4,5},{5,4},{6,7},{7,6},{8,9},{9,8},{10,11... | collective-permute-start | bytes 3342344 | tf_op jit(solution)/shard_map/ppermute | solution.py:275
  49.2 2.4 %collective-permute-start = (bf16[8,272,256]{2,1,0:T(8,128)(2,1)S(1)}, bf16[8,272,256]{2,1,0:T(8,128)(2,1)S(1)}, u32[]{:S(2)}, u32[]{:S(2)}) collective-permute-start(bf16[8,272,256]{2,1,0:T(8,128)(2,1)S(1)} %get-tuple-element.15), channel_id=1, source_target_pairs={{0,1},{1,0},{2,3},{3,2},{4,5},{5,4},{6,7},{7,6},{8,9},{9,8},{10,11... | collective-permute-start | bytes 3342344 | tf_op jit(solution)/shard_map/ppermute | solution.py:275
  51.6 0.3 collective-permute-done.1.part_ref
  51.9 3.1 %shard_map.52 = (f32[16,128]{1,0:T(8,128)S(1)}, f32[16,128]{1,0:T(8,128)S(1)}) custom-call(bf16[16,272,256]{2,1,0:T(8,128)(2,1)S(1)} %all_to_all.21.own_ref, bf16[8,272,256]{2,1,0:T(8,128)(2,1)S(1)} %collective-permute-done.1.part_ref), custom_call_target="tpu_custom_call" | custom-call | tf_op jit(solution)/shard_map/pallas_call | solution.py:229
  54.9 0.0 collective-permute-done.part_ref
  55.0 0.0 copy-start
  55.0 3.3 %shard_map.53 = (f32[16,16,128]{2,1,0:T(8,128)S(1)}, f32[16,128]{1,0:T(8,128)S(1)}) custom-call(bf16[16,272,256]{2,1,0:T(8,128)(2,1)S(1)} %all_to_all.21.own_ref, bf16[8,272,256]{2,1,0:T(8,128)(2,1)S(1)} %collective-permute-done.part_ref, f32[16,128]{1,0:T(8,128)S(1)} %get-tuple-element.8.refs_0_, f32[16,128]{1,0:T(8,128)S(1)} %get-tuple-element.9.refs_1_), custom_call_target="tpu_custom_call" | custom-call | tf_op jit(solution)/shard_map/pallas_call | solution.py:229
  58.3 32.8 %all_to_all.22.parts_ref = f32[16,16,128]{2,1,0:T(8,128)S(1)} all-to-all(f32[16,16,128]{2,1,0:T(8,128)S(1)} %get-tuple-element.10), channel_id=1, replica_groups={{0,8,16,24,32,40,48,56,64,72,80,88,96,104,112,120},{1,9,17,25,33,41,49,..., dimensions={0} | all-to-all | bytes 262144 | tf_op jit(solution)/shard_map/all_to_all | solution.py:295
  91.0 0.0 copy-done
  91.0 0.6 shard_map.54
  91.6 14.6 %all_to_all.23 = f32[32,1,128]{2,1,0:T(1,128)S(1)} all-to-all(f32[32,1,128]{2,1,0:T(1,128)S(1)} %bitcast.10), channel_id=1, replica_groups={{64,65,320,321,66,67,322,323,68,69,324,325,70,71,326,327,128,129,384,38..., dimensions={0} | all-to-all | bytes 32768 | tf_op jit(solution)/shard_map/all_to_all | solution.py:312
  106.2 0.5 shard_map.55
Async XLA Ops:
  47.2 4.6 %collective-permute-start.1 = (bf16[8,272,256]{2,1,0:T(8,128)(2,1)S(1)}, bf16[8,272,256]{2,1,0:T(8,128)(2,1)S(1)}, u32[]{:S(2)}, u32[]{:S(2)}) collective-permute-start(bf16[8,272,256]{2,1,0:T(8,128)(2,1)S(1)} %get-tuple-element.14), channel_id=1, source_target_pairs={{0,1},{1,0},{2,3},{3,2},{4,5},{5,4},{6,7},{7,6},{8,9},{9,8},{10,11... | collective-permute-start | bytes 3342344 | tf_op jit(solution)/shard_map/ppermute | solution.py:275
  49.2 5.8 %collective-permute-start = (bf16[8,272,256]{2,1,0:T(8,128)(2,1)S(1)}, bf16[8,272,256]{2,1,0:T(8,128)(2,1)S(1)}, u32[]{:S(2)}, u32[]{:S(2)}) collective-permute-start(bf16[8,272,256]{2,1,0:T(8,128)(2,1)S(1)} %get-tuple-element.15), channel_id=1, source_target_pairs={{0,1},{1,0},{2,3},{3,2},{4,5},{5,4},{6,7},{7,6},{8,9},{9,8},{10,11... | collective-permute-start | bytes 3342344 | tf_op jit(solution)/shard_map/ppermute | solution.py:275
  55.0 36.1 %copy-start = (f32[128]{0:T(128)S(1)}, f32[128]{0:T(128)}, u32[]{:S(2)}) copy-start(f32[128]{0:T(128)} %param.5) | copy-start | bytes 1540

commit v6 on v5

--- a/solution.py
+++ b/solution.py
@@ -115,17 +115,19 @@
     near = mass + quarter - least <= 200.0
     shift = jnp.where(near, least + 90.0, 0.0)
 
-    row = lax.broadcasted_iota(jnp.int32, (TAIL, LOCAL), 0)
+    row = lax.broadcasted_iota(jnp.int32, (TAIL, 2 * LOCAL), 0)
+    start = lax.broadcasted_iota(jnp.int32, (TAIL, 2 * LOCAL), 1) // LOCAL * 8
+    pick = jnp.where((row >= start) & (row < start + 3), 1.0, 0.0).astype(jnp.bfloat16)
     columns = column_ref.shape[0]
     for block in range(columns):
-        for side in range(2):
-            pick = (row >= 8 * side) & (row < 8 * side + 3)
-            offsets[block, side * LOCAL : (side + 1) * LOCAL] = lax.dot_general(
-                column_ref[block, own, :LOCAL],
-                jnp.where(pick, 1.0, 0.0).astype(jnp.bfloat16),
-                (((0,), (0,)), ((), ())),
-                preferred_element_type=jnp.float32,
-            ) - shift
+        both = lax.dot_general(
+            column_ref[block, own, :LOCAL],
+            pick,
+            (((0,), (0,)), ((), ())),
+            preferred_element_type=jnp.float32,
+        ) - shift
+        offsets[block, :LOCAL] = both[:, :LOCAL]
+        offsets[block, LOCAL:] = both[:, LOCAL:]
 
     def scores(block, mine):
         inner = lax.dot_general(

time: 107 us -> 106 us (level)
    all_to_all x1, blocking collectives: 14.6 us -> 13.4 us  [per_device(): lax.all_to_all(change, AXES, 0, 0, tiled=True, axis_index_groups=remainin...]
where the time goes in v6:
time: 106 us
  blocking collectives  91 us (86%)
  Pallas kernels  9.13 us (9%)
  starting transfers between devices  4.33 us (4%)
    all_to_all x1, blocking collectives, per_device(): lax.all_to_all(message, AXES, 0, 0, tiled=True, axis_index_groups=row_gro...  36 us
    all_to_all x1, blocking collectives, per_device(): lax.all_to_all(sums, AXES, 0, 0, tiled=True, axis_index_groups=row_groups...  32.9 us
    all_to_all x1, blocking collectives, per_device(): lax.all_to_all(change, AXES, 0, 0, tiled=True, axis_index_groups=remainin...  13.4 us
    pallas_call x6, Pallas kernels, call(): pl.pallas_call(kernel, out_shape=outs, compiler_params=pltpu.CompilerPara...  9.13 us
    all_gather x1, blocking collectives, per_device(): lax.all_gather(packed, 'narrow', axis=0, tiled=True, axis_index_groups=[[...  8.64 us
    ppermute x2, starting transfers between devices, per_device(): lax.ppermute(part, 'narrow', other_core)  4.33 us
  transfers between devices with their start and end apart: 2, of which 1 were waited for; matrix products, arithmetic and copies ran while one was open for 0% of the time, Pallas kernels for 3%

profile of v6, /device:TPU:1, one launch (start us, length us, event | category | flops | bytes accessed | tf_op | source)
XLA Modules:
  0.0 105.6 jit_solution(7081419032585522041)
XLA Ops:
  0.6 1.7 %shard_map.50 = bf16[144,256]{1,0:T(8,128)(2,1)} custom-call(bf16[128,256]{1,0:T(8,128)(2,1)} %points_ref.1, f32[1,128]{1,0:T(1,128)} %bitcast.13, f32[1,128]{1,0:T(1,128)} %bitcast.11), custom_call_target="tpu_custom_call" | custom-call | tf_op jit(solution)/shard_map/pallas_call | solution.py:231
  2.3 8.6 %all_gather.3.pair_ref = bf16[288,256]{1,0:T(8,128)(2,1)S(1)} all-gather(bf16[144,256]{1,0:T(8,128)(2,1)} %shard_map.50), channel_id=1, replica_groups={{0,1},{2,3},{4,5},{6,7},{8,9},{10,11},{12,13},{14,15},{16,17},{18,19},{..., dimensions={0}, use_global_device_ids=true | all-gather | bytes 221184 | tf_op jit(solution)/shard_map/all_gather | solution.py:258
  10.9 0.1 shard_map.51
  11.1 36.0 %all_to_all.21.own_ref = bf16[16,272,256]{2,1,0:T(8,128)(2,1)S(1)} all-to-all(bf16[16,272,256]{2,1,0:T(8,128)(2,1)S(1)} %shard_map.51), channel_id=1, replica_groups={{0,8,16,24,32,40,48,56,64,72,80,88,96,104,112,120},{256,264,272,280,288..., dimensions={0} | all-to-all | bytes 4456448 | tf_op jit(solution)/shard_map/all_to_all | solution.py:268
  47.1 0.1 fusion
  47.2 1.9 %collective-permute-start.1 = (bf16[8,272,256]{2,1,0:T(8,128)(2,1)S(1)}, bf16[8,272,256]{2,1,0:T(8,128)(2,1)S(1)}, u32[]{:S(2)}, u32[]{:S(2)}) collective-permute-start(bf16[8,272,256]{2,1,0:T(8,128)(2,1)S(1)} %get-tuple-element.14), channel_id=1, source_target_pairs={{0,1},{1,0},{2,3},{3,2},{4,5},{5,4},{6,7},{7,6},{8,9},{9,8},{10,11... | collective-permute-start | bytes 3342344 | tf_op jit(solution)/shard_map/ppermute | solution.py:277
  49.2 2.4 %collective-permute-start = (bf16[8,272,256]{2,1,0:T(8,128)(2,1)S(1)}, bf16[8,272,256]{2,1,0:T(8,128)(2,1)S(1)}, u32[]{:S(2)}, u32[]{:S(2)}) collective-permute-start(bf16[8,272,256]{2,1,0:T(8,128)(2,1)S(1)} %get-tuple-element.15), channel_id=1, source_target_pairs={{0,1},{1,0},{2,3},{3,2},{4,5},{5,4},{6,7},{7,6},{8,9},{9,8},{10,11... | collective-permute-start | bytes 3342344 | tf_op jit(solution)/shard_map/ppermute | solution.py:277
  51.6 0.3 collective-permute-done.1.part_ref
  51.9 3.0 %shard_map.52 = (f32[16,128]{1,0:T(8,128)S(1)}, f32[16,128]{1,0:T(8,128)S(1)}) custom-call(bf16[16,272,256]{2,1,0:T(8,128)(2,1)S(1)} %all_to_all.21.own_ref, bf16[8,272,256]{2,1,0:T(8,128)(2,1)S(1)} %collective-permute-done.1.part_ref), custom_call_target="tpu_custom_call" | custom-call | tf_op jit(solution)/shard_map/pallas_call | solution.py:231
  54.9 0.0 collective-permute-done.part_ref
  54.9 0.0 copy-start
  54.9 3.2 %shard_map.53 = (f32[16,16,128]{2,1,0:T(8,128)S(1)}, f32[16,128]{1,0:T(8,128)S(1)}) custom-call(bf16[16,272,256]{2,1,0:T(8,128)(2,1)S(1)} %all_to_all.21.own_ref, bf16[8,272,256]{2,1,0:T(8,128)(2,1)S(1)} %collective-permute-done.part_ref, f32[16,128]{1,0:T(8,128)S(1)} %get-tuple-element.8.refs_0_, f32[16,128]{1,0:T(8,128)S(1)} %get-tuple-element.9.refs_1_), custom_call_target="tpu_custom_call" | custom-call | tf_op jit(solution)/shard_map/pallas_call | solution.py:231
  58.2 32.9 %all_to_all.22.parts_ref = f32[16,16,128]{2,1,0:T(8,128)S(1)} all-to-all(f32[16,16,128]{2,1,0:T(8,128)S(1)} %get-tuple-element.10), channel_id=1, replica_groups={{0,8,16,24,32,40,48,56,64,72,80,88,96,104,112,120},{1,9,17,25,33,41,49,..., dimensions={0} | all-to-all | bytes 262144 | tf_op jit(solution)/shard_map/all_to_all | solution.py:297
  91.1 0.0 copy-done
  91.1 0.6 shard_map.54
  91.6 13.4 %all_to_all.23 = f32[32,1,128]{2,1,0:T(1,128)S(1)} all-to-all(f32[32,1,128]{2,1,0:T(1,128)S(1)} %bitcast.10), channel_id=1, replica_groups={{64,65,320,321,66,67,322,323,68,69,324,325,70,71,326,327,128,129,384,38..., dimensions={0} | all-to-all | bytes 32768 | tf_op jit(solution)/shard_map/all_to_all | solution.py:314
  105.1 0.5 shard_map.55
Async XLA Ops:
  47.2 4.6 %collective-permute-start.1 = (bf16[8,272,256]{2,1,0:T(8,128)(2,1)S(1)}, bf16[8,272,256]{2,1,0:T(8,128)(2,1)S(1)}, u32[]{:S(2)}, u32[]{:S(2)}) collective-permute-start(bf16[8,272,256]{2,1,0:T(8,128)(2,1)S(1)} %get-tuple-element.14), channel_id=1, source_target_pairs={{0,1},{1,0},{2,3},{3,2},{4,5},{5,4},{6,7},{7,6},{8,9},{9,8},{10,11... | collective-permute-start | bytes 3342344 | tf_op jit(solution)/shard_map/ppermute | solution.py:277
  49.2 5.7 %collective-permute-start = (bf16[8,272,256]{2,1,0:T(8,128)(2,1)S(1)}, bf16[8,272,256]{2,1,0:T(8,128)(2,1)S(1)}, u32[]{:S(2)}, u32[]{:S(2)}) collective-permute-start(bf16[8,272,256]{2,1,0:T(8,128)(2,1)S(1)} %get-tuple-element.15), channel_id=1, source_target_pairs={{0,1},{1,0},{2,3},{3,2},{4,5},{5,4},{6,7},{7,6},{8,9},{9,8},{10,11... | collective-permute-start | bytes 3342344 | tf_op jit(solution)/shard_map/ppermute | solution.py:277
  54.9 36.2 %copy-start = (f32[128]{0:T(128)S(1)}, f32[128]{0:T(128)}, u32[]{:S(2)}) copy-start(f32[128]{0:T(128)} %param.5) | copy-start | bytes 1540

commit v7 on v6

--- a/solution.py
+++ b/solution.py
@@ -15,8 +15,9 @@
 MEMBERS = 16
 LOCAL = 128
 TAIL = 16
-TILE = 4
+TILE = 2
 MESSAGE = 2 * LOCAL + TAIL
+FIRST = 6
 MIB = 1024 * 1024
 PAIRS = ((0, 1), (2, 3))
 CROSS = ((1, 2), (3, 0))
@@ -177,7 +178,6 @@
     else:
         sum_ref, base_ref, offsets = refs
     where = lax.axis_index("narrow") & 1
-    half = MEMBERS // 2
 
     def store(value, base):
         base_ref[...] = base
@@ -197,16 +197,16 @@
     @pl.when(where == 1)
     def _():
         value, base = log_sums(part_ref, own_ref, 1, offsets)
-        missing = jnp.full(value.shape, -1e30, jnp.float32)
+        missing = jnp.full((MEMBERS - value.shape[0], LOCAL), -1e30, jnp.float32)
         if final:
             store(
                 jnp.concatenate([missing, value], axis=0),
-                jnp.concatenate([base_before[:half], base], axis=0),
+                jnp.concatenate([base_before[:FIRST], base], axis=0),
             )
         else:
             store(
                 jnp.concatenate([value, missing], axis=0),
-                jnp.concatenate([base, base], axis=0),
+                jnp.concatenate([base, missing], axis=0),
             )
 
 
@@ -274,7 +274,7 @@
         axis_index_groups=row_groups([0]) + column_groups([1]),
     )
     other_core = [(at, at ^ 1) for at in range(narrow)]
-    halves = [lax.ppermute(part, "narrow", other_core) for part in jnp.split(own, 2)]
+    halves = [lax.ppermute(part, "narrow", other_core) for part in jnp.split(own, [FIRST])]
     offsets = [pltpu.VMEM((MEMBERS, 2 * LOCAL, LOCAL), jnp.float32)]
     lines = shape(MEMBERS, LOCAL)
     before = call(

time: 106 us -> 122 us (1.15)
  blocking collectives: 91 us -> 105 us
  waiting for transfers between devices: 0.31 us -> 1.96 us
    all_to_all x1, blocking collectives: 32.9 us -> 45.5 us  [per_device(): lax.all_to_all(sums, AXES, 0, 0, tiled=True, axis_index_groups=row_groups...]
    ppermute x2, waiting for transfers between devices: 0.31 us -> 1.96 us  [per_device(): lax.ppermute(part, 'narrow', other_core)]
    all_to_all x1, blocking collectives: 13.4 us -> 14.7 us  [per_device(): lax.all_to_all(change, AXES, 0, 0, tiled=True, axis_index_groups=remainin...]
  transfers between devices with their start and end apart: 2 -> 2, of which waited for: 1 -> 1; matrix products, arithmetic and copies ran while one was open for 0% -> 0% of each run, Pallas kernels for 3% -> 2%
where the time goes in v7:
time: 122 us; the launch traced here: 121 us
  blocking collectives  105 us (86%)
  Pallas kernels  9.43 us (8%)
  starting transfers between devices  4.33 us (4%)
  waiting for transfers between devices  1.96 us (2%)
    all_to_all x1, blocking collectives, per_device(): lax.all_to_all(sums, AXES, 0, 0, tiled=True, axis_index_groups=row_groups...  45.5 us
    all_to_all x1, blocking collectives, per_device(): lax.all_to_all(message, AXES, 0, 0, tiled=True, axis_index_groups=row_gro...  36 us
    all_to_all x1, blocking collectives, per_device(): lax.all_to_all(change, AXES, 0, 0, tiled=True, axis_index_groups=remainin...  14.7 us
    pallas_call x6, Pallas kernels, call(): pl.pallas_call(kernel, out_shape=outs, compiler_params=pltpu.CompilerPara...  9.43 us
    all_gather x1, blocking collectives, per_device(): lax.all_gather(packed, 'narrow', axis=0, tiled=True, axis_index_groups=[[...  8.64 us
    ppermute x2, starting transfers between devices, per_device(): lax.ppermute(part, 'narrow', other_core)  4.33 us
  transfers between devices with their start and end apart: 2, of which 1 were waited for; matrix products, arithmetic and copies ran while one was open for 0% of the time, Pallas kernels for 2%

profile of v7, /device:TPU:1, one launch (start us, length us, event | category | flops | bytes accessed | tf_op | source)
XLA Modules:
  0.0 121.4 jit_solution(1128207269057682303)
XLA Ops:
  0.6 1.7 %shard_map.50 = bf16[144,256]{1,0:T(8,128)(2,1)} custom-call(bf16[128,256]{1,0:T(8,128)(2,1)} %points_ref.1, f32[1,128]{1,0:T(1,128)} %bitcast.13, f32[1,128]{1,0:T(1,128)} %bitcast.11), custom_call_target="tpu_custom_call" | custom-call | tf_op jit(solution)/shard_map/pallas_call | solution.py:231
  2.3 8.6 %all_gather.3.pair_ref = bf16[288,256]{1,0:T(8,128)(2,1)S(1)} all-gather(bf16[144,256]{1,0:T(8,128)(2,1)} %shard_map.50), channel_id=1, replica_groups={{0,1},{2,3},{4,5},{6,7},{8,9},{10,11},{12,13},{14,15},{16,17},{18,19},{..., dimensions={0}, use_global_device_ids=true | all-gather | bytes 221184 | tf_op jit(solution)/shard_map/all_gather | solution.py:258
  10.9 0.1 shard_map.51
  11.1 36.0 %all_to_all.21.own_ref = bf16[16,272,256]{2,1,0:T(8,128)(2,1)S(1)} all-to-all(bf16[16,272,256]{2,1,0:T(8,128)(2,1)S(1)} %shard_map.51), channel_id=1, replica_groups={{0,8,16,24,32,40,48,56,64,72,80,88,96,104,112,120},{256,264,272,280,288..., dimensions={0} | all-to-all | bytes 4456448 | tf_op jit(solution)/shard_map/all_to_all | solution.py:268
  47.1 0.1 split.8
  47.2 1.9 %collective-permute-start = (bf16[10,272,256]{2,1,0:T(8,128)(2,1)S(1)}, bf16[10,272,256]{2,1,0:T(8,128)(2,1)S(1)}, u32[]{:S(2)}, u32[]{:S(2)}) collective-permute-start(bf16[10,272,256]{2,1,0:T(8,128)(2,1)S(1)} %split.8), channel_id=1, source_target_pairs={{0,1},{1,0},{2,3},{3,2},{4,5},{5,4},{6,7},{7,6},{8,9},{9,8},{10,11... | collective-permute-start | bytes 4177928 | tf_op jit(solution)/shard_map/ppermute | solution.py:277
  49.1 0.1 split.9
  49.2 2.4 %collective-permute-start.1 = (bf16[6,272,256]{2,1,0:T(8,128)(2,1)S(1)}, bf16[6,272,256]{2,1,0:T(8,128)(2,1)S(1)}, u32[]{:S(2)}, u32[]{:S(2)}) collective-permute-start(bf16[6,272,256]{2,1,0:T(8,128)(2,1)S(1)} %split.9), channel_id=1, source_target_pairs={{0,1},{1,0},{2,3},{3,2},{4,5},{5,4},{6,7},{7,6},{8,9},{9,8},{10,11... | collective-permute-start | bytes 2506760 | tf_op jit(solution)/shard_map/ppermute | solution.py:277
  51.6 2.0 %collective-permute-done.1.part_ref = bf16[6,272,256]{2,1,0:T(8,128)(2,1)S(1)} collective-permute-done((bf16[6,272,256]{2,1,0:T(8,128)(2,1)S(1)}, bf16[6,272,256]{2,1,0:T(8,128)(2,1)S(1)}, u32[]{:S(2)}, u32[]{:S(2)}) %collective-permute-start.1) | collective-permute-done | bytes 835616 | tf_op jit(solution)/shard_map/ppermute | solution.py:277
  53.5 2.5 %shard_map.52 = (f32[16,128]{1,0:T(8,128)S(1)}, f32[16,128]{1,0:T(8,128)S(1)}) custom-call(bf16[16,272,256]{2,1,0:T(8,128)(2,1)S(1)} %all_to_all.21.own_ref, bf16[6,272,256]{2,1,0:T(8,128)(2,1)S(1)} %collective-permute-done.1.part_ref), custom_call_target="tpu_custom_call" | custom-call | tf_op jit(solution)/shard_map/pallas_call | solution.py:231
  56.1 0.0 copy-start
  56.1 0.0 collective-permute-done.part_ref
  56.1 4.0 %shard_map.53 = (f32[16,16,128]{2,1,0:T(8,128)S(1)}, f32[16,128]{1,0:T(8,128)S(1)}) custom-call(bf16[16,272,256]{2,1,0:T(8,128)(2,1)S(1)} %all_to_all.21.own_ref, bf16[10,272,256]{2,1,0:T(8,128)(2,1)S(1)} %collective-permute-done.part_ref, f32[16,128]{1,0:T(8,128)S(1)} %get-tuple-element.8.refs_0_, f32[16,128]{1,0:T(8,128)S(1)} %get-tuple-element.9.refs_1_), custom_call_target="tpu_custom_call" | custom-call | tf_op jit(solution)/shard_map/pallas_call | solution.py:231
  60.1 45.5 %all_to_all.22.parts_ref = f32[16,16,128]{2,1,0:T(8,128)S(1)} all-to-all(f32[16,16,128]{2,1,0:T(8,128)S(1)} %get-tuple-element.10), channel_id=1, replica_groups={{0,8,16,24,32,40,48,56,64,72,80,88,96,104,112,120},{1,9,17,25,33,41,49,..., dimensions={0} | all-to-all | bytes 262144 | tf_op jit(solution)/shard_map/all_to_all | solution.py:297
  105.6 0.0 copy-done
  105.6 0.6 shard_map.54
  106.1 14.7 %all_to_all.23 = f32[32,1,128]{2,1,0:T(1,128)S(1)} all-to-all(f32[32,1,128]{2,1,0:T(1,128)S(1)} %bitcast.10), channel_id=1, replica_groups={{64,65,320,321,66,67,322,323,68,69,324,325,70,71,326,327,128,129,384,38..., dimensions={0} | all-to-all | bytes 32768 | tf_op jit(solution)/shard_map/all_to_all | solution.py:314
  120.9 0.5 shard_map.55
Async XLA Ops:
  47.2 8.9 %collective-permute-start = (bf16[10,272,256]{2,1,0:T(8,128)(2,1)S(1)}, bf16[10,272,256]{2,1,0:T(8,128)(2,1)S(1)}, u32[]{:S(2)}, u32[]{:S(2)}) collective-permute-start(bf16[10,272,256]{2,1,0:T(8,128)(2,1)S(1)} %split.8), channel_id=1, source_target_pairs={{0,1},{1,0},{2,3},{3,2},{4,5},{5,4},{6,7},{7,6},{8,9},{9,8},{10,11... | collective-permute-start | bytes 4177928 | tf_op jit(solution)/shard_map/ppermute | solution.py:277
  49.2 4.4 %collective-permute-start.1 = (bf16[6,272,256]{2,1,0:T(8,128)(2,1)S(1)}, bf16[6,272,256]{2,1,0:T(8,128)(2,1)S(1)}, u32[]{:S(2)}, u32[]{:S(2)}) collective-permute-start(bf16[6,272,256]{2,1,0:T(8,128)(2,1)S(1)} %split.9), channel_id=1, source_target_pairs={{0,1},{1,0},{2,3},{3,2},{4,5},{5,4},{6,7},{7,6},{8,9},{9,8},{10,11... | collective-permute-start | bytes 2506760 | tf_op jit(solution)/shard_map/ppermute | solution.py:277
  56.1 49.5 %copy-start = (f32[128]{0:T(128)S(1)}, f32[128]{0:T(128)}, u32[]{:S(2)}) copy-start(f32[128]{0:T(128)} %param.5) | copy-start | bytes 1540

commit v8 on v6

--- a/solution.py
+++ b/solution.py
@@ -31,27 +31,27 @@
 
 def row_groups(cores):
     return [
+        [index(x, y, z, core) for x in pair for z in range(8)]
+        for pair in PAIRS
+        for y in range(8)
+        for core in cores
+    ]
+
+
+def column_groups(cores):
+    return [
         [index(x, y, z, core) for x in pair for y in range(8)]
-        for pair in PAIRS
+        for pair in CROSS
         for z in range(8)
         for core in cores
     ]
 
 
-def column_groups(cores):
-    return [
-        [index(x, y, z, core) for x in pair for z in range(8)]
-        for pair in CROSS
-        for y in range(8)
-        for core in cores
-    ]
-
-
 def remaining_groups():
     return [
-        [index(x, y, z, core) for x in pair for z in range(8) for core in range(2)]
+        [index(x, y, z, core) for x in pair for y in range(8) for core in range(2)]
         for pair in CROSS
-        for y in range(8)
+        for z in range(8)
     ]
 
 
@@ -215,8 +215,11 @@
     top = jnp.max(parts, axis=0)
     value = top + jnp.log2(jnp.sum(jnp.exp2(parts - top[None]), axis=0))
     change = base_ref[...] - (2.0 * LN2) * value
+    wide, narrow = lax.axis_index("wide"), lax.axis_index("narrow")
+    z = 2 * (narrow >> 1) + (wide >> 5)
+    place = 8 * ((wide >> 3) & 1) + z
     row = lax.broadcasted_iota(jnp.int32, change.shape, 0)
-    mine = jnp.sum(jnp.where(row == lax.axis_index("wide") & (MEMBERS - 1), change, 0.0), axis=0, keepdims=True)
+    mine = jnp.sum(jnp.where(row == place, change, 0.0), axis=0, keepdims=True)
     new_ref[...] = potential_ref[...] + 0.5 * mine
     whole = jnp.sum(jnp.sum(change * change, axis=0, keepdims=True), axis=1, keepdims=True)
     change_ref[...] = jnp.broadcast_to(whole, change_ref.shape)

time: 106 us -> 107 us (level)
  starting transfers between devices: 4.33 us -> 8.08 us
  blocking collectives: 91 us -> 87.9 us
    ppermute x2, starting transfers between devices: 4.33 us -> 8.08 us  [per_device(): lax.ppermute(part, 'narrow', other_core)]
    all_to_all x1, blocking collectives: 36 us -> 32.8 us  [per_device(): lax.all_to_all(message, AXES, 0, 0, tiled=True, axis_index_groups=row_gro...]
where the time goes in v8:
time: 107 us; the launch traced here: 106 us
  blocking collectives  87.9 us (82%)
  Pallas kernels  9.13 us (9%)
  starting transfers between devices  8.08 us (8%)
    all_to_all x1, blocking collectives, per_device(): lax.all_to_all(message, AXES, 0, 0, tiled=True, axis_index_groups=row_gro...  32.8 us
    all_to_all x1, blocking collectives, per_device(): lax.all_to_all(sums, AXES, 0, 0, tiled=True, axis_index_groups=row_groups...  32.3 us
    all_to_all x1, blocking collectives, per_device(): lax.all_to_all(change, AXES, 0, 0, tiled=True, axis_index_groups=remainin...  14.2 us
    pallas_call x6, Pallas kernels, call(): pl.pallas_call(kernel, out_shape=outs, compiler_params=pltpu.CompilerPara...  9.13 us
    all_gather x1, blocking collectives, per_device(): lax.all_gather(packed, 'narrow', axis=0, tiled=True, axis_index_groups=[[...  8.64 us
    ppermute x2, starting transfers between devices, per_device(): lax.ppermute(part, 'narrow', other_core)  8.08 us
  transfers between devices with their start and end apart: 2, of which 1 were waited for; matrix products, arithmetic and copies ran while one was open for 0% of the time, Pallas kernels for 3%

profile of v8, /device:TPU:1, one launch (start us, length us, event | category | flops | bytes accessed | tf_op | source)
XLA Modules:
  0.0 106.4 jit_solution(4836892664883043331)
XLA Ops:
  0.6 1.7 %shard_map.50 = bf16[144,256]{1,0:T(8,128)(2,1)} custom-call(bf16[128,256]{1,0:T(8,128)(2,1)} %points_ref.1, f32[1,128]{1,0:T(1,128)} %bitcast.13, f32[1,128]{1,0:T(1,128)} %bitcast.11), custom_call_target="tpu_custom_call" | custom-call | tf_op jit(solution)/shard_map/pallas_call | solution.py:234
  2.3 8.6 %all_gather.3.pair_ref = bf16[288,256]{1,0:T(8,128)(2,1)S(1)} all-gather(bf16[144,256]{1,0:T(8,128)(2,1)} %shard_map.50), channel_id=1, replica_groups={{0,1},{2,3},{4,5},{6,7},{8,9},{10,11},{12,13},{14,15},{16,17},{18,19},{..., dimensions={0}, use_global_device_ids=true | all-gather | bytes 221184 | tf_op jit(solution)/shard_map/all_gather | solution.py:261
  10.9 0.1 shard_map.51
  11.1 32.8 %all_to_all.21.own_ref = bf16[16,272,256]{2,1,0:T(8,128)(2,1)S(1)} all-to-all(bf16[16,272,256]{2,1,0:T(8,128)(2,1)S(1)} %shard_map.51), channel_id=1, replica_groups={{0,256,2,258,4,260,6,262,64,320,66,322,68,324,70,326},{8,264,10,266,12,..., dimensions={0} | all-to-all | bytes 4456448 | tf_op jit(solution)/shard_map/all_to_all | solution.py:271
  43.9 0.1 fusion
  44.0 6.2 %collective-permute-start.1 = (bf16[8,272,256]{2,1,0:T(8,128)(2,1)S(1)}, bf16[8,272,256]{2,1,0:T(8,128)(2,1)S(1)}, u32[]{:S(2)}, u32[]{:S(2)}) collective-permute-start(bf16[8,272,256]{2,1,0:T(8,128)(2,1)S(1)} %get-tuple-element.14), channel_id=1, source_target_pairs={{0,1},{1,0},{2,3},{3,2},{4,5},{5,4},{6,7},{7,6},{8,9},{9,8},{10,11... | collective-permute-start | bytes 3342344 | tf_op jit(solution)/shard_map/ppermute | solution.py:280
  50.2 1.9 %collective-permute-start = (bf16[8,272,256]{2,1,0:T(8,128)(2,1)S(1)}, bf16[8,272,256]{2,1,0:T(8,128)(2,1)S(1)}, u32[]{:S(2)}, u32[]{:S(2)}) collective-permute-start(bf16[8,272,256]{2,1,0:T(8,128)(2,1)S(1)} %get-tuple-element.15), channel_id=1, source_target_pairs={{0,1},{1,0},{2,3},{3,2},{4,5},{5,4},{6,7},{7,6},{8,9},{9,8},{10,11... | collective-permute-start | bytes 3342344 | tf_op jit(solution)/shard_map/ppermute | solution.py:280
  52.1 0.4 collective-permute-done.1.part_ref
  52.6 3.0 %shard_map.52 = (f32[16,128]{1,0:T(8,128)S(1)}, f32[16,128]{1,0:T(8,128)S(1)}) custom-call(bf16[16,272,256]{2,1,0:T(8,128)(2,1)S(1)} %all_to_all.21.own_ref, bf16[8,272,256]{2,1,0:T(8,128)(2,1)S(1)} %collective-permute-done.1.part_ref), custom_call_target="tpu_custom_call" | custom-call | tf_op jit(solution)/shard_map/pallas_call | solution.py:234
  55.6 0.0 collective-permute-done.part_ref
  55.6 0.0 copy-start
  55.6 3.2 %shard_map.53 = (f32[16,16,128]{2,1,0:T(8,128)S(1)}, f32[16,128]{1,0:T(8,128)S(1)}) custom-call(bf16[16,272,256]{2,1,0:T(8,128)(2,1)S(1)} %all_to_all.21.own_ref, bf16[8,272,256]{2,1,0:T(8,128)(2,1)S(1)} %collective-permute-done.part_ref, f32[16,128]{1,0:T(8,128)S(1)} %get-tuple-element.8.refs_0_, f32[16,128]{1,0:T(8,128)S(1)} %get-tuple-element.9.refs_1_), custom_call_target="tpu_custom_call" | custom-call | tf_op jit(solution)/shard_map/pallas_call | solution.py:234
  58.8 32.3 %all_to_all.22.parts_ref = f32[16,16,128]{2,1,0:T(8,128)S(1)} all-to-all(f32[16,16,128]{2,1,0:T(8,128)S(1)} %get-tuple-element.10), channel_id=1, replica_groups={{0,256,2,258,4,260,6,262,64,320,66,322,68,324,70,326},{1,257,3,259,5,26..., dimensions={0} | all-to-all | bytes 262144 | tf_op jit(solution)/shard_map/all_to_all | solution.py:300
  91.1 0.0 copy-done
  91.1 0.6 shard_map.54
  91.7 14.2 %all_to_all.23 = f32[32,1,128]{2,1,0:T(1,128)S(1)} all-to-all(f32[32,1,128]{2,1,0:T(1,128)S(1)} %bitcast.10), channel_id=1, replica_groups={{64,65,72,73,80,81,88,89,96,97,104,105,112,113,120,121,128,129,136,137,..., dimensions={0} | all-to-all | bytes 32768 | tf_op jit(solution)/shard_map/all_to_all | solution.py:317
  105.9 0.5 shard_map.55
Async XLA Ops:
  44.0 8.5 %collective-permute-start.1 = (bf16[8,272,256]{2,1,0:T(8,128)(2,1)S(1)}, bf16[8,272,256]{2,1,0:T(8,128)(2,1)S(1)}, u32[]{:S(2)}, u32[]{:S(2)}) collective-permute-start(bf16[8,272,256]{2,1,0:T(8,128)(2,1)S(1)} %get-tuple-element.14), channel_id=1, source_target_pairs={{0,1},{1,0},{2,3},{3,2},{4,5},{5,4},{6,7},{7,6},{8,9},{9,8},{10,11... | collective-permute-start | bytes 3342344 | tf_op jit(solution)/shard_map/ppermute | solution.py:280
  50.2 5.4 %collective-permute-start = (bf16[8,272,256]{2,1,0:T(8,128)(2,1)S(1)}, bf16[8,272,256]{2,1,0:T(8,128)(2,1)S(1)}, u32[]{:S(2)}, u32[]{:S(2)}) collective-permute-start(bf16[8,272,256]{2,1,0:T(8,128)(2,1)S(1)} %get-tuple-element.15), channel_id=1, source_target_pairs={{0,1},{1,0},{2,3},{3,2},{4,5},{5,4},{6,7},{7,6},{8,9},{9,8},{10,11... | collective-permute-start | bytes 3342344 | tf_op jit(solution)/shard_map/ppermute | solution.py:280
  55.6 35.5 %copy-start = (f32[128]{0:T(128)S(1)}, f32[128]{0:T(128)}, u32[]{:S(2)}) copy-start(f32[128]{0:T(128)} %param.5) | copy-start | bytes 1540
